TPU v7x, 128 devices: a whole 4x4x4 slice. The times are simulated.
128 devices in a mesh: dp: 4 (over z_hi, core), ctx: 32 (over z_lo, x, y).
Axes of the slice: x: 4, y: 4, z: 4 (z_hi: 2, z_lo: 2; z = z_hi * 2 + z_lo), core: 2. Of those that a mesh axis runs over, the one named last changes fastest.
Arguments:
- query: bfloat16 [4, 7168, 2560], P('dp', 'ctx'), may hold values from -12 to 12
- keys: bfloat16 [4, 7168, 512], P('dp', 'ctx'), may hold values from -12 to 12
- values: bfloat16 [4, 7168, 512], P('dp', 'ctx'), may hold values from -6 to 6
- section_order: int32 [64], replicated, may hold values from 0 to 63, each once
- kept_sections: int32 [4, 64], P('dp'), may hold values 0 or 1
- segment_ids: int32 [4, 7168], P('dp'), may hold values from 0 to 2, never falling along the last dimension, each value on 1 to 3584 neighbouring positions
- out_weight: bfloat16 [2560, 5120], P('ctx', 'dp'), may hold values from -0.59765625 to 0.59765625
Outputs:
- projected: bfloat16 [4, 7168, 5120], P('dp', 'ctx')
All inputs are finite; a program needn't handle non-finite values. No bound on the sum of `kept_sections` on one device may be relied on, other than what follows from the above.
Results may differ from a plain program's by a relative error of at most 0.0085.
Values may be sent and summed in bfloat16 or wider, within the bound.
No kernel may reach another device: no remote copies, remote signals or barrier semaphores. Data moves between devices by JAX's collectives and lax.ppermute only.
A program may use at most 192 MiB of HBM per device.

v0:
```python
import functools
import math

import jax
import jax.numpy as jnp
from jax import lax
from jax.experimental import pallas as pl
from jax.experimental.pallas import tpu as pltpu
from jax.sharding import Mesh, PartitionSpec as P

HD = 128
RING = 4
SHIFTS = (0, -1, 1, 2)
BLOCK_KEYS = 512
ROW_TILE = 16


def shifted(array, axis, step, size=RING):
    return lax.ppermute(array, axis, [(i, (i + step) % size) for i in range(size)])


def ring_gather(array):
    def on(axis):
        half = array.shape[0] // 2
        from_left = shifted(array, axis, 1)
        from_right = shifted(array, axis, -1)
        far_head = shifted(from_left[:half], axis, 1)
        far_tail = shifted(from_right[half:], axis, -1)
        return array, from_left, from_right, far_head, far_tail

    return on


def wrap(value):
    return lax.rem(value + RING, RING)


def attention_kernel(
    groups, sec, nsec, max_range, coords, order, kept, starts, *refs
):
    q_refs, kv_refs, out_refs = refs[:4], refs[4:14], refs[14:18]
    k_all, v_all, scores, acc, peak, sem = refs[18:]
    zl, x, y = coords[0], coords[1], coords[2]
    rows = nsec * sec
    factor = math.log2(math.e) / math.sqrt(HD)
    q_rows = groups * sec

    def copies(act):
        for side in range(2):
            own_zl = zl if side == 0 else 1 - zl
            base = side * 5
            for x_rel in range(4):
                abs_x = wrap(x + SHIFTS[x_rel])
                for y_rel in range(4):
                    abs_y = wrap(y + SHIFTS[y_rel])
                    if x_rel < 3:
                        source = kv_refs[base + x_rel].at[y_rel]
                    else:
                        source = kv_refs[base + 3 + y_rel // 2].at[y_rel % 2]
                    for part in range(2):
                        section = ((own_zl * RING + abs_x) * RING + abs_y) * 2 + part
                        at = pl.multiple_of(order[section] * sec, ROW_TILE)
                        act(source.at[pl.ds(part * sec, sec), pl.ds(0, HD)], k_all.at[pl.ds(at, sec), :])
                        act(source.at[pl.ds(part * sec, sec), pl.ds(HD, HD)], v_all.at[pl.ds(at, sec), pl.ds(0, HD)])

    copies(lambda a, b: pltpu.make_async_copy(a, b, sem).start())
    pad = k_all.shape[0] - rows
    k_all[pl.ds(rows, pad), :] = jnp.zeros((pad, HD), k_all.dtype)
    v_all[pl.ds(rows, pad), pl.ds(0, HD)] = jnp.zeros((pad, HD), v_all.dtype)
    v_all[:, pl.ds(HD, HD)] = jnp.ones((k_all.shape[0], HD), v_all.dtype)
    copies(lambda a, b: pltpu.make_async_copy(a, b, sem).wait())

    first, second = starts[0], starts[1]

    def segment_start(pos):
        return jnp.where(pos >= second, second, jnp.where(pos >= first, first, 0))

    for piece in range(4):
        abs_y = wrap(y + SHIFTS[piece])
        q_ref, out_ref = q_refs[piece], out_refs[piece]

        def one_section(part, _, q_ref=q_ref, out_ref=out_ref, abs_y=abs_y):
            section = ((zl * RING + x) * RING + abs_y) * 2 + part
            place = order[section]
            begin = place * sec
            own_rows = pl.ds(pl.multiple_of(part * sec, ROW_TILE), sec)

            @pl.when(kept[place] == 0)
            def _():
                out_ref[own_rows, :] = jnp.zeros((sec, groups * HD), out_ref.dtype)

            @pl.when(kept[place] != 0)
            def _():
                key_first = segment_start(begin) // ROW_TILE * ROW_TILE
                last_start = segment_start(begin + sec - 1)
                blocks = (begin + sec - key_first + BLOCK_KEYS - 1) // BLOCK_KEYS
                q_tile = jnp.concatenate(
                    [q_ref[own_rows, pl.ds(g * HD, HD)] for g in range(groups)], axis=0
                )
                peak[...] = jnp.full(peak.shape, -1e30, jnp.float32)

                def lane_max(block_scores):
                    best = peak[...]
                    for i in range(BLOCK_KEYS // HD):
                        best = jnp.maximum(best, block_scores[:, i * HD : (i + 1) * HD])
                    peak[...] = best

                def score(block, _):
                    at = pl.multiple_of(key_first + block * BLOCK_KEYS, ROW_TILE)
                    raw = lax.dot_general(
                        q_tile,
                        k_all[pl.ds(at, BLOCK_KEYS), :],
                        (((1,), (1,)), ((), ())),
                        preferred_element_type=jnp.float32,
                    )
                    masked = (at < last_start) | (at + BLOCK_KEYS > begin)

                    @pl.when(masked)
                    def _():
                        row_pos = begin + lax.rem(
                            lax.broadcasted_iota(jnp.int32, (q_rows, 1), 0), sec
                        )
                        row_start = segment_start(row_pos)
                        key_pos = at + lax.broadcasted_iota(jnp.int32, (1, BLOCK_KEYS), 1)
                        seen = (key_pos <= row_pos) & (key_pos >= row_start)
                        hidden = jnp.where(seen, raw, -1e30)
                        scores[block] = hidden
                        lane_max(hidden)

                    @pl.when(jnp.logical_not(masked))
                    def _():
                        scores[block] = raw
                        lane_max(raw)

                    return 0

                lax.fori_loop(0, blocks, score, 0)
                top = jnp.max(peak[...], axis=1, keepdims=True) * factor
                acc[...] = jnp.zeros(acc.shape, jnp.float32)

                def weigh(block, _):
                    at = pl.multiple_of(key_first + block * BLOCK_KEYS, ROW_TILE)
                    weights = jnp.exp2(scores[block] * factor - top).astype(jnp.bfloat16)
                    acc[...] += jnp.dot(
                        weights,
                        v_all[pl.ds(at, BLOCK_KEYS), :],
                        preferred_element_type=jnp.float32,
                    )
                    return 0

                lax.fori_loop(0, blocks, weigh, 0)
                result = (acc[:, pl.ds(0, HD)] / acc[:, pl.ds(HD, HD)]).astype(out_ref.dtype)
                for g in range(groups):
                    out_ref[own_rows, pl.ds(g * HD, HD)] = result[g * sec : (g + 1) * sec]

            return 0

        lax.fori_loop(0, 2, one_section, 0)


def attention(coords, order, kept, starts, q_pieces, kv_pieces, sec, nsec):
    groups = q_pieces[0].shape[1] // HD
    rows = nsec * sec
    max_range = rows // 2 + sec + ROW_TILE
    max_blocks = -(-max_range // BLOCK_KEYS)
    smem = pl.BlockSpec(memory_space=pltpu.SMEM)
    vmem = pl.BlockSpec(memory_space=pltpu.VMEM)
    return pl.pallas_call(
        functools.partial(attention_kernel, groups, sec, nsec, max_range),
        out_shape=[jax.ShapeDtypeStruct(q.shape, q.dtype) for q in q_pieces],
        in_specs=[smem] * 4 + [vmem] * 4 + [pl.BlockSpec(memory_space=pl.ANY)] * 10,
        out_specs=[vmem] * 4,
        scratch_shapes=[
            pltpu.VMEM((rows + BLOCK_KEYS, HD), jnp.bfloat16),
            pltpu.VMEM((rows + BLOCK_KEYS, 2 * HD), jnp.bfloat16),
            pltpu.VMEM((max_blocks, groups * sec, BLOCK_KEYS), jnp.float32),
            pltpu.VMEM((groups * sec, 2 * HD), jnp.float32),
            pltpu.VMEM((groups * sec, HD), jnp.float32),
            pltpu.SemaphoreType.DMA,
        ],
        compiler_params=pltpu.CompilerParams(vmem_limit_bytes=48 * 2**20),
        cost_estimate=pl.CostEstimate(
            flops=8 * 10**9, bytes_accessed=6 * 10**6, transcendentals=16 * 10**6
        ),
        name="attend",
    )(coords, order, kept, starts, *q_pieces, *kv_pieces)


def project_kernel(coords, core, *refs):
    att_refs, weights = refs[:8], refs[8]
    own_out, other_out, att = refs[9:]
    tok, wide = att_refs[0].shape

    @pl.when(pl.program_id(0) == 0)
    def _():
        for who in range(2):
            for j in range(4):
                head = wrap(coords[2] + SHIFTS[j])
                at = pl.multiple_of(head * wide, HD)
                att[pl.ds(who * tok, tok), pl.ds(at, wide)] = att_refs[4 * who + j][...]

    got = jnp.dot(att[...], weights[...], preferred_element_type=jnp.float32)
    got = got.astype(own_out.dtype)
    own_out[...] = got[:tok]
    other_out[...] = got[tok:]


def project(coords, core, own_att, other_att, weights, cols):
    tok, wide = own_att[0].shape
    rows = RING * wide
    split = 2
    step = cols // split
    piece = pl.BlockSpec((tok, wide), lambda i, *_: (0, 0))
    return pl.pallas_call(
        project_kernel,
        out_shape=[
            jax.ShapeDtypeStruct((tok, 4 * cols), jnp.bfloat16),
            jax.ShapeDtypeStruct((tok, 2 * cols), jnp.bfloat16),
        ],
        grid_spec=pltpu.PrefetchScalarGridSpec(
            num_scalar_prefetch=2,
            grid=(2 * split,),
            in_specs=[piece] * 8
            + [pl.BlockSpec((rows, step), lambda i, *_: (i // split, i % split))],
            out_specs=[
                pl.BlockSpec(
                    (tok, step),
                    lambda i, where, core: (0, (i // split * 2 + core[0]) * split + i % split),
                ),
                pl.BlockSpec((tok, step), lambda i, *_: (0, i)),
            ],
            scratch_shapes=[pltpu.VMEM((2 * tok, rows), jnp.bfloat16)],
        ),
        compiler_params=pltpu.CompilerParams(vmem_limit_bytes=48 * 2**20),
        cost_estimate=pl.CostEstimate(
            flops=6 * 10**9, bytes_accessed=18 * 10**6, transcendentals=0
        ),
        name="project",
    )(coords, core, *own_att, *other_att, weights)


def merge_kernel(core, whole, theirs, out):
    del core, whole
    out[...] = theirs[...]


def merge(core, whole, theirs, cols):
    tok = theirs.shape[0]
    return pl.pallas_call(
        merge_kernel,
        out_shape=jax.ShapeDtypeStruct(whole.shape, whole.dtype),
        grid_spec=pltpu.PrefetchScalarGridSpec(
            num_scalar_prefetch=1,
            grid=(2,),
            in_specs=[
                pl.BlockSpec(memory_space=pl.ANY),
                pl.BlockSpec((tok, cols), lambda i, core: (0, i)),
            ],
            out_specs=pl.BlockSpec((tok, cols), lambda i, core: (0, i * 2 + 1 - core[0])),
        ),
        input_output_aliases={1: 0},
        cost_estimate=pl.CostEstimate(flops=0, bytes_accessed=3 * 10**6, transcendentals=0),
        name="merge",
    )(core, whole, theirs)


def per_device(query, keys, values, section_order, kept_sections, segment_ids, out_weight):
    tok = query.shape[1]
    sec = tok // 2
    nsec = section_order.shape[0]
    core = lax.axis_index("c")
    zl, x, y = lax.axis_index("zl"), lax.axis_index("x"), lax.axis_index("y")
    coords = jnp.stack([zl, x, y]).astype(jnp.int32)
    starts = jnp.stack([jnp.sum(segment_ids[0] < 1), jnp.sum(segment_ids[0] < 2)]).astype(jnp.int32)

    def head_slice(array, shift):
        wide = array.shape[2] // RING
        return lax.dynamic_slice_in_dim(array[0], wrap(y + shift) * wide, wide, 1)

    kv_pieces, q_pieces = [], []
    for shift in SHIFTS:
        kv = jnp.concatenate([head_slice(keys, -shift), head_slice(values, -shift)], axis=1)
        kv_pieces.append(kv if shift == 0 else shifted(kv, "y", -shift))
    for shift in SHIFTS:
        q = head_slice(query, -shift)
        q_pieces.append(q if shift == 0 else shifted(q, "y", -shift))
    near = jnp.stack(kv_pieces)
    far = shifted(near, "zl", 1, 2)
    kv_all = ring_gather(near)("x") + ring_gather(far)("x")

    cols = out_weight.shape[1]
    weights = lax.all_gather(out_weight, ("zh", "zl", "x", "y"), axis=0, tiled=True)

    attended = attention(
        coords, section_order, kept_sections[0], starts, q_pieces, kv_all, sec, nsec
    )
    by_shift = dict(zip(SHIFTS, attended))
    back = {0: by_shift[0]}
    for shift in SHIFTS[1:]:
        back[wrap_static(-shift)] = shifted(by_shift[shift], "y", shift)
    own_att = [back[s] for s in SHIFTS]
    other_att = [shifted(a, "c", 1, 2) for a in own_att]
    which = core[None].astype(jnp.int32)
    whole, for_other = project(coords, which, own_att, other_att, weights, cols)
    return merge(which, whole, shifted(for_other, "c", 1, 2), cols)[None]


def wrap_static(shift):
    return 2 if shift in (2, -2) else shift


def solution(mesh):
    fine = Mesh(mesh.devices.reshape(2, 2, 2, 4, 4), ("zh", "c", "zl", "x", "y"))
    dp, ctx = ("zh", "c"), ("zl", "x", "y")
    return jax.shard_map(
        per_device,
        mesh=fine,
        in_specs=(
            P(dp, ctx, None),
            P(dp, ctx, None),
            P(dp, ctx, None),
            P(),
            P(dp, None),
            P(dp, None),
            P(ctx, dp),
        ),
        out_specs=P(dp, ctx, None),
        check_vma=False,
    )
```

profile of v0, /device:TPU:1, one launch (start us, length us, event | category | flops | bytes accessed | tf_op | source)
XLA Modules:
  0.0 148.4 jit_solution(6588453276908790181)
XLA Ops:
  8.4 2.2 %collective-permute-start.3 = (bf16[224,256]{1,0:T(8,128)(2,1)S(1)}, bf16[224,256]{1,0:T(8,128)(2,1)S(1)}, u32[]{:S(2)}, u32[]{:S(2)}) collective-permute-start(bf16[224,256]{1,0:T(8,128)(2,1)S(1)} %pad_maximum_fusion.1), channel_id=1, source_target_pairs={{0,1},{1,2},{2,3},{3,0},{4,5},{5,6},{6,7},{7,4},{8,9},{9,10},{10,1... | collective-permute-start | bytes 344072 | tf_op jit(solution)/shard_map/ppermute | solution.py:19
  10.6 1.5 %collective-permute-start.4 = (bf16[224,256]{1,0:T(8,128)(2,1)S(1)}, bf16[224,256]{1,0:T(8,128)(2,1)S(1)}, u32[]{:S(2)}, u32[]{:S(2)}) collective-permute-start(bf16[224,256]{1,0:T(8,128)(2,1)S(1)} %pad_maximum_fusion.2), channel_id=1, source_target_pairs={{0,3},{1,0},{2,1},{3,2},{4,7},{5,4},{6,5},{7,6},{8,11},{9,8},{10,9... | collective-permute-start | bytes 344072 | tf_op jit(solution)/shard_map/ppermute | solution.py:19
  12.1 1.7 %collective-permute-start.5 = (bf16[224,256]{1,0:T(8,128)(2,1)S(1)}, bf16[224,256]{1,0:T(8,128)(2,1)S(1)}, u32[]{:S(2)}, u32[]{:S(2)}) collective-permute-start(bf16[224,256]{1,0:T(8,128)(2,1)S(1)} %pad_maximum_fusion.3), channel_id=1, source_target_pairs={{0,2},{1,3},{2,0},{3,1},{4,6},{5,7},{6,4},{7,5},{8,10},{9,11},{10,... | collective-permute-start | bytes 344072 | tf_op jit(solution)/shard_map/ppermute | solution.py:19
  14.7 3.5 %collective-permute-done.5 = bf16[224,256]{1,0:T(8,128)(2,1)S(1)} collective-permute-done((bf16[224,256]{1,0:T(8,128)(2,1)S(1)}, bf16[224,256]{1,0:T(8,128)(2,1)S(1)}, u32[]{:S(2)}, u32[]{:S(2)}) %collective-permute-start.5) | collective-permute-done | bytes 114720 | tf_op jit(solution)/shard_map/ppermute | solution.py:19
  18.3 1.6 %collective-permute-start.10 = (bf16[4,224,256]{2,1,0:T(8,128)(2,1)S(1)}, bf16[4,224,256]{2,1,0:T(8,128)(2,1)S(1)}, u32[]{:S(2)}, u32[]{:S(2)}) collective-permute-start(bf16[4,224,256]{2,1,0:T(8,128)(2,1)S(1)} %pad_maximum_fusion.refs_4_), channel_id=1, source_target_pairs={{0,16},{16,0},{1,17},{17,1},{2,18},{18,2},{3,19},{19,3},{4,20},{20... | collective-permute-start | bytes 1376264 | tf_op jit(solution)/shard_map/ppermute | solution.py:19
  21.1 1.5 collective-permute-start.7
  22.6 7.2 %collective-permute-done.10.refs_9_ = bf16[4,224,256]{2,1,0:T(8,128)(2,1)S(1)} collective-permute-done((bf16[4,224,256]{2,1,0:T(8,128)(2,1)S(1)}, bf16[4,224,256]{2,1,0:T(8,128)(2,1)S(1)}, u32[]{:S(2)}, u32[]{:S(2)}) %collective-permute-start.10) | collective-permute-done | bytes 458784 | tf_op jit(solution)/shard_map/ppermute | solution.py:19
  31.0 1.5 collective-permute-start.12
  32.4 2.0 %dynamic-slice_bitcast_fusion = (bf16[224,640]{1,0:T(8,128)(2,1)}, bf16[224,640]{1,0:T(8,128)(2,1)S(1)}, bf16[224,640]{1,0:T(8,128)(2,1)S(1)}, bf16[224,640]{1,0:T(8,128)(2,1)S(1)}) fusion(bf16[1,224,2560]{2,1,0:T(8,128)(2,1)} %param.7, s32[]{:T(128)S(6)} %select_n.31, s32[]{:T(128)S(6)} %select_n.29, s32[]{:T(128)S(6)} %select_n.28, s32[]{:T(128)S(6)} %select_n.30), kind=kLoop, calls=%fused_computation.1 | loop fusion | bytes 2293776 | tf_op jit(solution)/shard_map/dynamic_slice | solution.py:278
  34.6 2.7 %collective-permute-start.1 = (bf16[224,640]{1,0:T(8,128)(2,1)S(1)}, bf16[224,640]{1,0:T(8,128)(2,1)S(1)}, u32[]{:S(2)}, u32[]{:S(2)}) collective-permute-start(bf16[224,640]{1,0:T(8,128)(2,1)S(1)} %get-tuple-element.22), channel_id=1, source_target_pairs={{0,3},{1,0},{2,1},{3,2},{4,7},{5,4},{6,5},{7,6},{8,11},{9,8},{10,9... | collective-permute-start | bytes 860168 | tf_op jit(solution)/shard_map/ppermute | solution.py:19
  38.6 5.8 %collective-permute-done.11.refs_10_ = bf16[4,224,256]{2,1,0:T(8,128)(2,1)S(1)} collective-permute-done((bf16[4,224,256]{2,1,0:T(8,128)(2,1)S(1)}, bf16[4,224,256]{2,1,0:T(8,128)(2,1)S(1)}, u32[]{:S(2)}, u32[]{:S(2)}) %collective-permute-start.11) | collective-permute-done | bytes 458784 | tf_op jit(solution)/shard_map/ppermute | solution.py:19
  45.2 2.7 %collective-permute-start.9 = (bf16[2,224,256]{2,1,0:T(8,128)(2,1)}, bf16[2,224,256]{2,1,0:T(8,128)(2,1)}, u32[]{:S(2)}, u32[]{:S(2)}) collective-permute-start(bf16[2,224,256]{2,1,0:T(8,128)(2,1)} %slice.17), channel_id=1, source_target_pairs={{0,12},{4,0},{8,4},{12,8},{1,13},{5,1},{9,5},{13,9},{2,14},{6,2},{... | collective-permute-start | bytes 688136 | tf_op jit(solution)/shard_map/ppermute | solution.py:19
  49.3 2.7 %collective-permute-start.14 = (bf16[2,224,256]{2,1,0:T(8,128)(2,1)}, bf16[2,224,256]{2,1,0:T(8,128)(2,1)}, u32[]{:S(2)}, u32[]{:S(2)}) collective-permute-start(bf16[2,224,256]{2,1,0:T(8,128)(2,1)} %slice.19), channel_id=1, source_target_pairs={{0,12},{4,0},{8,4},{12,8},{1,13},{5,1},{9,5},{13,9},{2,14},{6,2},{... | collective-permute-start | bytes 688136 | tf_op jit(solution)/shard_map/ppermute | solution.py:19
  54.1 2.1 %collective-permute-done.8.refs_7_ = bf16[2,224,256]{2,1,0:T(8,128)(2,1)} collective-permute-done((bf16[2,224,256]{2,1,0:T(8,128)(2,1)}, bf16[2,224,256]{2,1,0:T(8,128)(2,1)}, u32[]{:S(2)}, u32[]{:S(2)}) %collective-permute-start.8) | collective-permute-done | bytes 229408 | tf_op jit(solution)/shard_map/ppermute | solution.py:19
  56.2 9.8 %collective-permute-done.13.refs_12_ = bf16[2,224,256]{2,1,0:T(8,128)(2,1)} collective-permute-done((bf16[2,224,256]{2,1,0:T(8,128)(2,1)}, bf16[2,224,256]{2,1,0:T(8,128)(2,1)}, u32[]{:S(2)}, u32[]{:S(2)}) %collective-permute-start.13) | collective-permute-done | bytes 229408 | tf_op jit(solution)/shard_map/ppermute | solution.py:19
  67.0 27.8 %attend.1 = (bf16[224,640]{1,0:T(8,128)(2,1)}, bf16[224,640]{1,0:T(8,128)(2,1)S(1)}, bf16[224,640]{1,0:T(8,128)(2,1)S(1)}, bf16[224,640]{1,0:T(8,128)(2,1)S(1)}) custom-call(s32[3]{0:T(128)S(1)} %pad_add_fusion.coords, s32[64]{0:T(128)S(1)} %copy-done.2, s32[64]{0:T(128)S(1)} %bitcast.37, s32[2]{0:T(128)S(1)} %pad_add_fusion.1.starts, ...), custom_call_target="tpu_custom_call" | custom-call | flops 8000000000 | bytes 6000000 | tf_op jit(solution)/shard_map/attend/pallas_call | solution.py:168
  95.0 2.7 %collective-permute-start.16 = (bf16[224,640]{1,0:T(8,128)(2,1)S(1)}, bf16[224,640]{1,0:T(8,128)(2,1)S(1)}, u32[]{:S(2)}, u32[]{:S(2)}) collective-permute-start(bf16[224,640]{1,0:T(8,128)(2,1)S(1)} %get-tuple-element.13), channel_id=1, source_target_pairs={{0,3},{1,0},{2,1},{3,2},{4,7},{5,4},{6,5},{7,6},{8,11},{9,8},{10,9... | collective-permute-start | bytes 860168 | tf_op jit(solution)/shard_map/ppermute | solution.py:19
  97.6 13.4 %collective-permute-done.15.refs_1_ = bf16[224,640]{1,0:T(8,128)(2,1)S(1)} collective-permute-done((bf16[224,640]{1,0:T(8,128)(2,1)S(1)}, bf16[224,640]{1,0:T(8,128)(2,1)S(1)}, u32[]{:S(2)}, u32[]{:S(2)}) %collective-permute-start.15) | collective-permute-done | bytes 286752 | tf_op jit(solution)/shard_map/ppermute | solution.py:19
  111.5 5.9 %collective-permute-done.17.refs_3_ = bf16[224,640]{1,0:T(8,128)(2,1)S(1)} collective-permute-done((bf16[224,640]{1,0:T(8,128)(2,1)S(1)}, bf16[224,640]{1,0:T(8,128)(2,1)S(1)}, u32[]{:S(2)}, u32[]{:S(2)}) %collective-permute-start.17) | collective-permute-done | bytes 286752 | tf_op jit(solution)/shard_map/ppermute | solution.py:19
  117.5 1.5 %collective-permute-done.21.refs_7_ = bf16[224,640]{1,0:T(8,128)(2,1)S(1)} collective-permute-done((bf16[224,640]{1,0:T(8,128)(2,1)S(1)}, bf16[224,640]{1,0:T(8,128)(2,1)S(1)}, u32[]{:S(2)}, u32[]{:S(2)}) %collective-permute-start.21) | collective-permute-done | bytes 286752 | tf_op jit(solution)/shard_map/ppermute | solution.py:19
  119.0 5.0 %all-gather.2.cloned.1.call-done.refs_8_ = bf16[5120,1280]{1,0:T(8,128)(2,1)} async-done(((bf16[80,1280]{1,0:T(8,128)(2,1)}), bf16[5120,1280]{1,0:T(8,128)(2,1)}) %all-gather.2.cloned.1.call-update) | async-done | bytes 13107216 | tf_op jit(solution)/shard_map/all_gather | solution.py:292
  124.0 11.4 %project.1 = (bf16[224,5120]{1,0:T(8,128)(2,1)}, bf16[224,2560]{1,0:T(8,128)(2,1)S(1)}) custom-call(s32[3]{0:T(128)S(1)} %pad_add_fusion.coords, s32[1]{0:T(128)} %bitcast.core, bf16[224,640]{1,0:T(8,128)(2,1)} %get-tuple-element.11.refs_0_, bf16[224,640]{1,0:T(8,128)(2,1)S(1)} %collective-permute-done.15.refs_1_, ...), custom_call_target="tpu_custom_call" | custom-call | flops 6000000000 | bytes 18000000 | tf_op jit(solution)/shard_map/project/pallas_call | solution.py:214
  136.0 2.4 %collective-permute-done.22.theirs = bf16[224,2560]{1,0:T(8,128)(2,1)S(1)} collective-permute-done((bf16[224,2560]{1,0:T(8,128)(2,1)S(1)}, bf16[224,2560]{1,0:T(8,128)(2,1)S(1)}, u32[]{:S(2)}, u32[]{:S(2)}) %collective-permute-start.22) | collective-permute-done | bytes 1146912 | tf_op jit(solution)/shard_map/ppermute | solution.py:19
  139.5 2.1 %merge.1 = bf16[224,5120]{1,0:T(8,128)(2,1)} custom-call(s32[1]{0:T(128)} %bitcast.core, bf16[224,5120]{1,0:T(8,128)(2,1)} %get-tuple-element.15.whole, bf16[224,2560]{1,0:T(8,128)(2,1)} %copy-done.4), custom_call_target="tpu_custom_call", output_to_operand_aliasing={{}: (1, {})} | custom-call | bytes 3000000 | tf_op jit(solution)/shard_map/merge/pallas_call | solution.py:249
  (54 shorter events, 14.2 us)
Async XLA Ops:
  6.5 117.5 %all-gather.2.cloned.1.call-start = ((), (), s32[]{:S(2)}) async-start(), calls=%async_computation | async-start | bytes 13312000 | tf_op jit(solution)/shard_map/all_gather | solution.py:292
  8.4 6.4 %collective-permute-start.3 = (bf16[224,256]{1,0:T(8,128)(2,1)S(1)}, bf16[224,256]{1,0:T(8,128)(2,1)S(1)}, u32[]{:S(2)}, u32[]{:S(2)}) collective-permute-start(bf16[224,256]{1,0:T(8,128)(2,1)S(1)} %pad_maximum_fusion.1), channel_id=1, source_target_pairs={{0,1},{1,2},{2,3},{3,0},{4,5},{5,6},{6,7},{7,4},{8,9},{9,10},{10,1... | collective-permute-start | bytes 344072 | tf_op jit(solution)/shard_map/ppermute | solution.py:19
  10.6 4.1 %collective-permute-start.4 = (bf16[224,256]{1,0:T(8,128)(2,1)S(1)}, bf16[224,256]{1,0:T(8,128)(2,1)S(1)}, u32[]{:S(2)}, u32[]{:S(2)}) collective-permute-start(bf16[224,256]{1,0:T(8,128)(2,1)S(1)} %pad_maximum_fusion.2), channel_id=1, source_target_pairs={{0,3},{1,0},{2,1},{3,2},{4,7},{5,4},{6,5},{7,6},{8,11},{9,8},{10,9... | collective-permute-start | bytes 344072 | tf_op jit(solution)/shard_map/ppermute | solution.py:19
  12.1 6.1 %collective-permute-start.5 = (bf16[224,256]{1,0:T(8,128)(2,1)S(1)}, bf16[224,256]{1,0:T(8,128)(2,1)S(1)}, u32[]{:S(2)}, u32[]{:S(2)}) collective-permute-start(bf16[224,256]{1,0:T(8,128)(2,1)S(1)} %pad_maximum_fusion.3), channel_id=1, source_target_pairs={{0,2},{1,3},{2,0},{3,1},{4,6},{5,7},{6,4},{7,5},{8,10},{9,11},{10,... | collective-permute-start | bytes 344072 | tf_op jit(solution)/shard_map/ppermute | solution.py:19
  18.3 11.5 %collective-permute-start.10 = (bf16[4,224,256]{2,1,0:T(8,128)(2,1)S(1)}, bf16[4,224,256]{2,1,0:T(8,128)(2,1)S(1)}, u32[]{:S(2)}, u32[]{:S(2)}) collective-permute-start(bf16[4,224,256]{2,1,0:T(8,128)(2,1)S(1)} %pad_maximum_fusion.refs_4_), channel_id=1, source_target_pairs={{0,16},{16,0},{1,17},{17,1},{2,18},{18,2},{3,19},{19,3},{4,20},{20... | collective-permute-start | bytes 1376264 | tf_op jit(solution)/shard_map/ppermute | solution.py:19
  19.9 14.6 %collective-permute-start.6 = (bf16[4,224,256]{2,1,0:T(8,128)(2,1)S(1)}, bf16[4,224,256]{2,1,0:T(8,128)(2,1)S(1)}, u32[]{:S(2)}, u32[]{:S(2)}) collective-permute-start(bf16[4,224,256]{2,1,0:T(8,128)(2,1)S(1)} %pad_maximum_fusion.refs_4_), channel_id=1, source_target_pairs={{0,4},{4,8},{8,12},{12,0},{1,5},{5,9},{9,13},{13,1},{2,6},{6,10},{... | collective-permute-start | bytes 1376264 | tf_op jit(solution)/shard_map/ppermute | solution.py:19
  21.1 16.8 %collective-permute-start.7 = (bf16[4,224,256]{2,1,0:T(8,128)(2,1)S(1)}, bf16[4,224,256]{2,1,0:T(8,128)(2,1)S(1)}, u32[]{:S(2)}, u32[]{:S(2)}) collective-permute-start(bf16[4,224,256]{2,1,0:T(8,128)(2,1)S(1)} %pad_maximum_fusion.refs_4_), channel_id=1, source_target_pairs={{0,12},{4,0},{8,4},{12,8},{1,13},{5,1},{9,5},{13,9},{2,14},{6,2},{... | collective-permute-start | bytes 1376264 | tf_op jit(solution)/shard_map/ppermute | solution.py:19
  29.8 14.7 %collective-permute-start.11 = (bf16[4,224,256]{2,1,0:T(8,128)(2,1)S(1)}, bf16[4,224,256]{2,1,0:T(8,128)(2,1)S(1)}, u32[]{:S(2)}, u32[]{:S(2)}) collective-permute-start(bf16[4,224,256]{2,1,0:T(8,128)(2,1)S(1)} %collective-permute-done.10.refs_9_), channel_id=1, source_target_pairs={{0,4},{4,8},{8,12},{12,0},{1,5},{5,9},{9,13},{13,1},{2,6},{6,10},{... | collective-permute-start | bytes 1376264 | tf_op jit(solution)/shard_map/ppermute | solution.py:19
  31.0 14.2 %collective-permute-start.12 = (bf16[4,224,256]{2,1,0:T(8,128)(2,1)S(1)}, bf16[4,224,256]{2,1,0:T(8,128)(2,1)S(1)}, u32[]{:S(2)}, u32[]{:S(2)}) collective-permute-start(bf16[4,224,256]{2,1,0:T(8,128)(2,1)S(1)} %collective-permute-done.10.refs_9_), channel_id=1, source_target_pairs={{0,12},{4,0},{8,4},{12,8},{1,13},{5,1},{9,5},{13,9},{2,14},{6,2},{... | collective-permute-start | bytes 1376264 | tf_op jit(solution)/shard_map/ppermute | solution.py:19
  34.5 14.1 %collective-permute-start = (bf16[224,640]{1,0:T(8,128)(2,1)S(1)}, bf16[224,640]{1,0:T(8,128)(2,1)S(1)}, u32[]{:S(2)}, u32[]{:S(2)}) collective-permute-start(bf16[224,640]{1,0:T(8,128)(2,1)S(1)} %get-tuple-element.20), channel_id=1, source_target_pairs={{0,1},{1,2},{2,3},{3,0},{4,5},{5,6},{6,7},{7,4},{8,9},{9,10},{10,1... | collective-permute-start | bytes 860168 | tf_op jit(solution)/shard_map/ppermute | solution.py:19
  34.6 14.0 %collective-permute-start.1 = (bf16[224,640]{1,0:T(8,128)(2,1)S(1)}, bf16[224,640]{1,0:T(8,128)(2,1)S(1)}, u32[]{:S(2)}, u32[]{:S(2)}) collective-permute-start(bf16[224,640]{1,0:T(8,128)(2,1)S(1)} %get-tuple-element.22), channel_id=1, source_target_pairs={{0,3},{1,0},{2,1},{3,2},{4,7},{5,4},{6,5},{7,6},{8,11},{9,8},{10,9... | collective-permute-start | bytes 860168 | tf_op jit(solution)/shard_map/ppermute | solution.py:19
  37.9 16.2 %collective-permute-start.2 = (bf16[224,640]{1,0:T(8,128)(2,1)}, bf16[224,640]{1,0:T(8,128)(2,1)}, u32[]{:S(2)}, u32[]{:S(2)}) collective-permute-start(bf16[224,640]{1,0:T(8,128)(2,1)} %get-tuple-element.19), channel_id=1, source_target_pairs={{0,2},{1,3},{2,0},{3,1},{4,6},{5,7},{6,4},{7,5},{8,10},{9,11},{10,... | collective-permute-start | bytes 860168 | tf_op jit(solution)/shard_map/ppermute | solution.py:19
  44.5 11.8 %collective-permute-start.8 = (bf16[2,224,256]{2,1,0:T(8,128)(2,1)}, bf16[2,224,256]{2,1,0:T(8,128)(2,1)}, u32[]{:S(2)}, u32[]{:S(2)}) collective-permute-start(bf16[2,224,256]{2,1,0:T(8,128)(2,1)} %slice.16), channel_id=1, source_target_pairs={{0,4},{4,8},{8,12},{12,0},{1,5},{5,9},{9,13},{13,1},{2,6},{6,10},{... | collective-permute-start | bytes 688136 | tf_op jit(solution)/shard_map/ppermute | solution.py:19
  45.2 11.0 %collective-permute-start.9 = (bf16[2,224,256]{2,1,0:T(8,128)(2,1)}, bf16[2,224,256]{2,1,0:T(8,128)(2,1)}, u32[]{:S(2)}, u32[]{:S(2)}) collective-permute-start(bf16[2,224,256]{2,1,0:T(8,128)(2,1)} %slice.17), channel_id=1, source_target_pairs={{0,12},{4,0},{8,4},{12,8},{1,13},{5,1},{9,5},{13,9},{2,14},{6,2},{... | collective-permute-start | bytes 688136 | tf_op jit(solution)/shard_map/ppermute | solution.py:19
  48.6 17.5 %collective-permute-start.13 = (bf16[2,224,256]{2,1,0:T(8,128)(2,1)}, bf16[2,224,256]{2,1,0:T(8,128)(2,1)}, u32[]{:S(2)}, u32[]{:S(2)}) collective-permute-start(bf16[2,224,256]{2,1,0:T(8,128)(2,1)} %slice.18), channel_id=1, source_target_pairs={{0,4},{4,8},{8,12},{12,0},{1,5},{5,9},{9,13},{13,1},{2,6},{6,10},{... | collective-permute-start | bytes 688136 | tf_op jit(solution)/shard_map/ppermute | solution.py:19
  49.3 16.8 %collective-permute-start.14 = (bf16[2,224,256]{2,1,0:T(8,128)(2,1)}, bf16[2,224,256]{2,1,0:T(8,128)(2,1)}, u32[]{:S(2)}, u32[]{:S(2)}) collective-permute-start(bf16[2,224,256]{2,1,0:T(8,128)(2,1)} %slice.19), channel_id=1, source_target_pairs={{0,12},{4,0},{8,4},{12,8},{1,13},{5,1},{9,5},{13,9},{2,14},{6,2},{... | collective-permute-start | bytes 688136 | tf_op jit(solution)/shard_map/ppermute | solution.py:19
  94.9 16.1 %collective-permute-start.15 = (bf16[224,640]{1,0:T(8,128)(2,1)S(1)}, bf16[224,640]{1,0:T(8,128)(2,1)S(1)}, u32[]{:S(2)}, u32[]{:S(2)}) collective-permute-start(bf16[224,640]{1,0:T(8,128)(2,1)S(1)} %get-tuple-element.12), channel_id=1, source_target_pairs={{0,1},{1,2},{2,3},{3,0},{4,5},{5,6},{6,7},{7,4},{8,9},{9,10},{10,1... | collective-permute-start | bytes 860168 | tf_op jit(solution)/shard_map/ppermute | solution.py:19
  95.0 16.0 %collective-permute-start.16 = (bf16[224,640]{1,0:T(8,128)(2,1)S(1)}, bf16[224,640]{1,0:T(8,128)(2,1)S(1)}, u32[]{:S(2)}, u32[]{:S(2)}) collective-permute-start(bf16[224,640]{1,0:T(8,128)(2,1)S(1)} %get-tuple-element.13), channel_id=1, source_target_pairs={{0,3},{1,0},{2,1},{3,2},{4,7},{5,4},{6,5},{7,6},{8,11},{9,8},{10,9... | collective-permute-start | bytes 860168 | tf_op jit(solution)/shard_map/ppermute | solution.py:19
  97.6 19.8 %collective-permute-start.17 = (bf16[224,640]{1,0:T(8,128)(2,1)S(1)}, bf16[224,640]{1,0:T(8,128)(2,1)S(1)}, u32[]{:S(2)}, u32[]{:S(2)}) collective-permute-start(bf16[224,640]{1,0:T(8,128)(2,1)S(1)} %get-tuple-element.14), channel_id=1, source_target_pairs={{0,2},{1,3},{2,0},{3,1},{4,6},{5,7},{6,4},{7,5},{8,10},{9,11},{10,... | collective-permute-start | bytes 860168 | tf_op jit(solution)/shard_map/ppermute | solution.py:19
  97.6 19.8 %collective-permute-start.18 = (bf16[224,640]{1,0:T(8,128)(2,1)}, bf16[224,640]{1,0:T(8,128)(2,1)S(1)}, u32[]{:S(2)}, u32[]{:S(2)}) collective-permute-start(bf16[224,640]{1,0:T(8,128)(2,1)} %get-tuple-element.11.refs_0_), channel_id=1, source_target_pairs={{0,32},{32,0},{1,33},{33,1},{2,34},{34,2},{3,35},{35,3},{4,36},{36... | collective-permute-start | bytes 860168 | tf_op jit(solution)/shard_map/ppermute | solution.py:19
  111.0 6.5 %collective-permute-start.19 = (bf16[224,640]{1,0:T(8,128)(2,1)S(1)}, bf16[224,640]{1,0:T(8,128)(2,1)S(1)}, u32[]{:S(2)}, u32[]{:S(2)}) collective-permute-start(bf16[224,640]{1,0:T(8,128)(2,1)S(1)} %collective-permute-done.15.refs_1_), channel_id=1, source_target_pairs={{0,32},{32,0},{1,33},{33,1},{2,34},{34,2},{3,35},{35,3},{4,36},{36... | collective-permute-start | bytes 860168 | tf_op jit(solution)/shard_map/ppermute | solution.py:19
  111.0 6.5 %collective-permute-start.20 = (bf16[224,640]{1,0:T(8,128)(2,1)S(1)}, bf16[224,640]{1,0:T(8,128)(2,1)S(1)}, u32[]{:S(2)}, u32[]{:S(2)}) collective-permute-start(bf16[224,640]{1,0:T(8,128)(2,1)S(1)} %collective-permute-done.16.refs_2_), channel_id=1, source_target_pairs={{0,32},{32,0},{1,33},{33,1},{2,34},{34,2},{3,35},{35,3},{4,36},{36... | collective-permute-start | bytes 860168 | tf_op jit(solution)/shard_map/ppermute | solution.py:19
  117.4 1.6 %collective-permute-start.21 = (bf16[224,640]{1,0:T(8,128)(2,1)S(1)}, bf16[224,640]{1,0:T(8,128)(2,1)S(1)}, u32[]{:S(2)}, u32[]{:S(2)}) collective-permute-start(bf16[224,640]{1,0:T(8,128)(2,1)S(1)} %collective-permute-done.17.refs_3_), channel_id=1, source_target_pairs={{0,32},{32,0},{1,33},{33,1},{2,34},{34,2},{3,35},{35,3},{4,36},{36... | collective-permute-start | bytes 860168 | tf_op jit(solution)/shard_map/ppermute | solution.py:19
  135.4 3.1 %collective-permute-start.22 = (bf16[224,2560]{1,0:T(8,128)(2,1)S(1)}, bf16[224,2560]{1,0:T(8,128)(2,1)S(1)}, u32[]{:S(2)}, u32[]{:S(2)}) collective-permute-start(bf16[224,2560]{1,0:T(8,128)(2,1)S(1)} %get-tuple-element.16), channel_id=1, source_target_pairs={{0,32},{32,0},{1,33},{33,1},{2,34},{34,2},{3,35},{35,3},{4,36},{36... | collective-permute-start | bytes 3440648 | tf_op jit(solution)/shard_map/ppermute | solution.py:19
  (6 other events, 83.3 us)
Sparse Core Ops, SparseCore 0:
  10.2 113.7 all-gather.1
where the time goes:
time: 149 us; the launch traced here: 148 us
  waiting for transfers between devices  58.3 us (39%)
  Pallas kernels  41.3 us (28%)
  starting transfers between devices  24.4 us (16%)
  between operations  13.5 us (9%)
  local copies, waits for them, and re-layouts  8.61 us (6%)
  other arithmetic  2.27 us (2%)
    ppermute x23, waiting for transfers between devices, shifted(): lax.ppermute(array, axis, [(i, (i + step) % size) for i in range(size)])  52.6 us
    pallas_call x1, Pallas kernels, attention(): pl.pallas_call(functools.partial(attention_kernel, groups, sec, nsec, max...  27.8 us
    ppermute x23, starting transfers between devices, shifted(): lax.ppermute(array, axis, [(i, (i + step) % size) for i in range(size)])  24.4 us
    pallas_call x1, Pallas kernels, project(): pl.pallas_call(project_kernel, out_shape=[jax.ShapeDtypeStruct((tok, 4 *...  11.4 us
    all_gather x1, waiting for transfers between devices, per_device(): lax.all_gather(out_weight, ('zh', 'zl', 'x', 'y'), axis=0, tiled=True)  4.97 us
    dynamic_slice x2, local copies, waits for them, and re-layouts, head_slice(): return lax.dynamic_slice_in_dim(array[0], wrap(y + shift) * wide, wide, 1)  3.11 us
  transfers between devices with their start and end apart: 24, of which 11 were waited for; matrix products, arithmetic and copies ran while one was open for 6% of the time, Pallas kernels for 19%

commit v1 on v0

v1 whole, which is shorter than its diff:
```python
import functools
import math

import jax
import jax.numpy as jnp
from jax import lax
from jax.experimental import pallas as pl
from jax.experimental.pallas import tpu as pltpu
from jax.sharding import Mesh, PartitionSpec as P

HD = 128
RING = 4
SHIFTS = (0, -1, 1, 2)
BLOCK_KEYS = 2048
TAIL_STEP = 256
ROW_TILE = 16


def shifted(array, axis, step, size=RING):
    return lax.ppermute(array, axis, [(i, (i + step) % size) for i in range(size)])


def ring_gather(array):
    def on(axis):
        half = array.shape[0] // 2
        from_left = shifted(array, axis, 1)
        from_right = shifted(array, axis, -1)
        far_head = shifted(from_left[:half], axis, 1)
        far_tail = shifted(from_right[half:], axis, -1)
        return array, from_left, from_right, far_head, far_tail

    return on


def wrap(value):
    return lax.rem(value + RING, RING)


def attention_kernel(
    groups, sec, nsec, coords, order, kept, starts, *refs
):
    q_refs, kv_refs, out_refs = refs[:4], refs[4:14], refs[14:18]
    held, q_all, out_all, acc, peak, sem = refs[18:]
    zl, x, y = coords[0], coords[1], coords[2]
    rows = nsec * sec
    factor = math.log2(math.e) / math.sqrt(HD)

    def copies(act):
        for side in range(2):
            own_zl = zl if side == 0 else 1 - zl
            base = side * 5
            for x_rel in range(4):
                abs_x = wrap(x + SHIFTS[x_rel])
                for y_rel in range(4):
                    abs_y = wrap(y + SHIFTS[y_rel])
                    if x_rel < 3:
                        source = kv_refs[base + x_rel].at[y_rel]
                    else:
                        source = kv_refs[base + 3 + y_rel // 2].at[y_rel % 2]
                    for part in range(2):
                        section = ((own_zl * RING + abs_x) * RING + abs_y) * 2 + part
                        at = pl.multiple_of(order[section] * sec, ROW_TILE)
                        act(
                            source.at[pl.ds(part * sec, sec), :],
                            held.at[pl.ds(at, sec), pl.ds(0, 2 * HD)],
                        )

    copies(lambda a, b: pltpu.make_async_copy(a, b, sem).start())
    pad = held.shape[0] - rows
    held[pl.ds(rows, pad), pl.ds(0, 2 * HD)] = jnp.zeros((pad, 2 * HD), held.dtype)
    held[:, pl.ds(2 * HD, HD)] = jnp.ones((held.shape[0], HD), held.dtype)
    copies(lambda a, b: pltpu.make_async_copy(a, b, sem).wait())

    first, second = starts[0], starts[1]

    def segment_start(pos):
        return jnp.where(pos >= second, second, jnp.where(pos >= first, first, 0))

    for piece in range(4):
        q_all[pl.ds(piece * 2 * sec, 2 * sec), :] = q_refs[piece][...]

    def one_section(index, _):
        piece, part = index // 2, lax.rem(index, 2)
        shift = jnp.where(piece == 1, -1, jnp.where(piece == 0, 0, piece - 1))
        section = ((zl * RING + x) * RING + wrap(y + shift)) * 2 + part
        place = order[section]
        begin = place * sec
        own_rows = pl.ds(pl.multiple_of(index * sec, ROW_TILE), sec)

        @pl.when(kept[place] == 0)
        def _():
            out_all[own_rows, :] = jnp.zeros((sec, groups * HD), out_all.dtype)

        @pl.when(kept[place] != 0)
        def _():
            key_first = segment_start(begin) // ROW_TILE * ROW_TILE
            last_start = segment_start(begin + sec - 1)
            full = (begin + sec - key_first) // BLOCK_KEYS
            tail_first = key_first + full * BLOCK_KEYS
            tail_steps = (begin + sec - tail_first + TAIL_STEP - 1) // TAIL_STEP
            peak[...] = jnp.full(peak.shape, -1e30, jnp.float32)
            acc[...] = jnp.zeros(acc.shape, jnp.float32)

            def step(first, width, masked):
                at = pl.multiple_of(first, ROW_TILE)
                keys = held[pl.ds(at, width), pl.ds(0, HD)]
                values = held[pl.ds(at, width), pl.ds(HD, 2 * HD)]
                if masked:
                    row_pos = begin + lax.broadcasted_iota(jnp.int32, (sec, 1), 0)
                    row_start = segment_start(row_pos)
                    key_pos = at + lax.broadcasted_iota(jnp.int32, (1, width), 1)
                    seen = (key_pos <= row_pos) & (key_pos >= row_start)
                def score(g):
                    got = lax.dot_general(
                        q_all[own_rows, pl.ds(g * HD, HD)],
                        keys,
                        (((1,), (1,)), ((), ())),
                        preferred_element_type=jnp.float32,
                    )
                    return jnp.where(seen, got, -1e30) if masked else got

                def weigh(g, got):
                    rows_g = pl.ds(g * sec, sec)
                    before = peak[rows_g, :]
                    top = jnp.maximum(before, jnp.max(got, axis=1, keepdims=True))
                    peak[rows_g, :] = top
                    scaled = top * factor
                    weights = jnp.exp2(
                        got * factor - jnp.concatenate([scaled] * (width // HD), axis=1)
                    ).astype(jnp.bfloat16)
                    return weights, jnp.exp2(before * factor - scaled)

                def add(g, weights, rescale):
                    rows_g = pl.ds(g * sec, sec)
                    acc[rows_g, :] = acc[rows_g, :] * jnp.concatenate(
                        [rescale, rescale], axis=1
                    ) + jnp.dot(weights, values, preferred_element_type=jnp.float32)

                ahead = score(0)
                waiting = None
                for g in range(groups):
                    got, ahead = ahead, score(g + 1) if g + 1 < groups else None
                    if waiting is not None:
                        add(g - 1, *waiting)
                    waiting = weigh(g, got)
                add(groups - 1, *waiting)

            def full_block(block, _):
                first = key_first + block * BLOCK_KEYS
                masked = (first < last_start) | (first + BLOCK_KEYS > begin)
                pl.when(masked)(lambda: step(first, BLOCK_KEYS, True))
                pl.when(jnp.logical_not(masked))(lambda: step(first, BLOCK_KEYS, False))
                return 0

            lax.fori_loop(0, full, full_block, 0)
            for steps in range(1, BLOCK_KEYS // TAIL_STEP + 1):
                pl.when(tail_steps == steps)(
                    lambda steps=steps: step(tail_first, steps * TAIL_STEP, True)
                )
            for g in range(groups):
                rows_g = pl.ds(g * sec, sec)
                out_all[own_rows, pl.ds(g * HD, HD)] = (
                    acc[rows_g, pl.ds(0, HD)] / acc[rows_g, pl.ds(HD, HD)]
                ).astype(out_all.dtype)

        return 0

    lax.fori_loop(0, 8, one_section, 0)
    for piece in range(4):
        out_refs[piece][...] = out_all[pl.ds(piece * 2 * sec, 2 * sec), :]


def attention(coords, order, kept, starts, q_pieces, kv_pieces, sec, nsec):
    groups = q_pieces[0].shape[1] // HD
    rows = nsec * sec
    smem = pl.BlockSpec(memory_space=pltpu.SMEM)
    vmem = pl.BlockSpec(memory_space=pltpu.VMEM)
    return pl.pallas_call(
        functools.partial(attention_kernel, groups, sec, nsec),
        out_shape=[jax.ShapeDtypeStruct(q.shape, q.dtype) for q in q_pieces],
        in_specs=[smem] * 4 + [vmem] * 4 + [pl.BlockSpec(memory_space=pl.ANY)] * 10,
        out_specs=[vmem] * 4,
        scratch_shapes=[
            pltpu.VMEM((rows + TAIL_STEP, 3 * HD), jnp.bfloat16),
            pltpu.VMEM((8 * sec, groups * HD), jnp.bfloat16),
            pltpu.VMEM((8 * sec, groups * HD), jnp.bfloat16),
            pltpu.VMEM((groups * sec, 2 * HD), jnp.float32),
            pltpu.VMEM((groups * sec, HD), jnp.float32),
            pltpu.SemaphoreType.DMA,
        ],
        compiler_params=pltpu.CompilerParams(vmem_limit_bytes=48 * 2**20),
        cost_estimate=pl.CostEstimate(
            flops=8 * 10**9, bytes_accessed=6 * 10**6, transcendentals=16 * 10**6
        ),
        name="attend",
    )(coords, order, kept, starts, *q_pieces, *kv_pieces)


def project_kernel(coords, core, *refs):
    att_refs, weights = refs[:8], refs[8]
    own_out, other_out, att = refs[-3:]
    tok, wide = att_refs[0].shape

    @pl.when(pl.program_id(0) == 0)
    def _():
        for who in range(2):
            for j in range(4):
                head = wrap(coords[2] + SHIFTS[j])
                at = pl.multiple_of(head * wide, HD)
                att[pl.ds(who * tok, tok), pl.ds(at, wide)] = att_refs[4 * who + j][...]

    got = jnp.dot(att[...], weights[...], preferred_element_type=jnp.float32)
    got = got.astype(own_out.dtype)
    own_out[...] = got[:tok]
    other_out[...] = got[tok:]


def project(coords, core, own_att, other_att, weights, cols, half, whole):
    tok, wide = own_att[0].shape
    rows = RING * wide
    step = 2 * HD
    steps = cols // step
    piece = pl.BlockSpec((tok, wide), lambda i, *_: (0, 0))
    given = [] if whole is None else [whole]
    return pl.pallas_call(
        project_kernel,
        out_shape=[
            jax.ShapeDtypeStruct((tok, 4 * cols), jnp.bfloat16),
            jax.ShapeDtypeStruct((tok, cols), jnp.bfloat16),
        ],
        grid_spec=pltpu.PrefetchScalarGridSpec(
            num_scalar_prefetch=2,
            grid=(steps,),
            in_specs=[piece] * 8
            + [pl.BlockSpec((rows, step), lambda i, *_: (half, i))]
            + [pl.BlockSpec(memory_space=pl.ANY)] * len(given),
            out_specs=[
                pl.BlockSpec(
                    (tok, step), lambda i, where, core: (0, (half * 2 + core[0]) * steps + i)
                ),
                pl.BlockSpec((tok, step), lambda i, *_: (0, i)),
            ],
            scratch_shapes=[pltpu.VMEM((2 * tok, rows), jnp.bfloat16)],
        ),
        input_output_aliases={11: 0} if given else {},
        compiler_params=pltpu.CompilerParams(vmem_limit_bytes=48 * 2**20),
        cost_estimate=pl.CostEstimate(
            flops=3 * 10**9, bytes_accessed=9 * 10**6, transcendentals=0
        ),
        name="project",
    )(coords, core, *own_att, *other_att, weights, *given)


def merge_kernel(core, first, second, whole, out):
    del core, whole

    @pl.when(pl.program_id(0) == 0)
    def _():
        out[...] = first[...]

    @pl.when(pl.program_id(0) == 1)
    def _():
        out[...] = second[...]


def merge(core, theirs, whole):
    tok, cols = theirs[0].shape
    return pl.pallas_call(
        merge_kernel,
        out_shape=jax.ShapeDtypeStruct(whole.shape, whole.dtype),
        grid_spec=pltpu.PrefetchScalarGridSpec(
            num_scalar_prefetch=1,
            grid=(2,),
            in_specs=[pl.BlockSpec((tok, cols), lambda i, core: (0, 0))] * 2
            + [pl.BlockSpec(memory_space=pl.ANY)],
            out_specs=pl.BlockSpec((tok, cols), lambda i, core: (0, i * 2 + 1 - core[0])),
        ),
        input_output_aliases={3: 0},
        cost_estimate=pl.CostEstimate(flops=0, bytes_accessed=3 * 10**6, transcendentals=0),
        name="merge",
    )(core, *theirs, whole)


def per_device(query, keys, values, section_order, kept_sections, segment_ids, out_weight):
    tok = query.shape[1]
    sec = tok // 2
    nsec = section_order.shape[0]
    core = lax.axis_index("c")
    zl, x, y = lax.axis_index("zl"), lax.axis_index("x"), lax.axis_index("y")
    coords = jnp.stack([zl, x, y]).astype(jnp.int32)
    starts = jnp.stack([jnp.sum(segment_ids[0] < 1), jnp.sum(segment_ids[0] < 2)]).astype(jnp.int32)

    def head_slice(array, shift):
        wide = array.shape[2] // RING
        return lax.dynamic_slice_in_dim(array[0], wrap(y + shift) * wide, wide, 1)

    kv_pieces, q_pieces = [], []
    for shift in SHIFTS:
        kv = jnp.concatenate([head_slice(keys, -shift), head_slice(values, -shift)], axis=1)
        kv_pieces.append(kv if shift == 0 else shifted(kv, "y", -shift))
    for shift in SHIFTS:
        q = head_slice(query, -shift)
        q_pieces.append(q if shift == 0 else shifted(q, "y", -shift))
    near = jnp.stack(kv_pieces)
    far = shifted(near, "zl", 1, 2)
    kv_all = ring_gather(near)("x") + ring_gather(far)("x")

    cols = out_weight.shape[1]
    weights = lax.all_gather(out_weight, ("zh", "zl", "x", "y"), axis=0, tiled=True)

    attended = attention(
        coords, section_order, kept_sections[0], starts, q_pieces, kv_all, sec, nsec
    )
    by_shift = dict(zip(SHIFTS, attended))
    back = {0: by_shift[0]}
    for shift in SHIFTS[1:]:
        back[wrap_static(-shift)] = shifted(by_shift[shift], "y", shift)
    own_att = [back[s] for s in SHIFTS]
    other_att = [shifted(a, "c", 1, 2) for a in own_att]
    which = core[None].astype(jnp.int32)
    whole, theirs = None, []
    for half in range(2):
        whole, for_other = project(
            coords, which, own_att, other_att, weights, cols, half, whole
        )
        theirs.append(shifted(for_other, "c", 1, 2))
    return merge(which, theirs, whole)[None]


def wrap_static(shift):
    return 2 if shift in (2, -2) else shift


def solution(mesh):
    fine = Mesh(mesh.devices.reshape(2, 2, 2, 4, 4), ("zh", "c", "zl", "x", "y"))
    dp, ctx = ("zh", "c"), ("zl", "x", "y")
    return jax.shard_map(
        per_device,
        mesh=fine,
        in_specs=(
            P(dp, ctx, None),
            P(dp, ctx, None),
            P(dp, ctx, None),
            P(),
            P(dp, None),
            P(dp, None),
            P(ctx, dp),
        ),
        out_specs=P(dp, ctx, None),
        check_vma=False,
    )
```

time: 149 us -> 153 us (1.027)
  starting transfers between devices: 24.4 us -> 58.4 us
  waiting for transfers between devices: 58.3 us -> 37.4 us
  Pallas kernels: 41.3 us -> 28.7 us
  local copies, waits for them, and re-layouts: 8.61 us -> 11.9 us
    ppermute x23 -> x24, starting transfers between devices: 24.4 us -> 58.4 us  [shifted(): lax.ppermute(array, axis, [(i, (i + step) % size) for i in range(size)])]
    ppermute x23 -> x24, waiting for transfers between devices: 52.6 us -> 30 us  [shifted(): lax.ppermute(array, axis, [(i, (i + step) % size) for i in range(size)])]
    pallas_call x1, Pallas kernels: 27.8 us -> 11.1 us  [attention(): pl.pallas_call(functools.partial(attention_kernel, groups, sec, nsec), ou...]
    pallas_call x1 -> x2, Pallas kernels: 11.4 us -> 15.4 us  [project(): pl.pallas_call(project_kernel, out_shape=[jax.ShapeDtypeStruct((tok, 4 *...]
    unnamed x12 -> x22, local copies, waits for them, and re-layouts: 2.67 us -> 5.9 us
    all_gather x1, waiting for transfers between devices: 4.97 us -> 6.66 us  [per_device(): lax.all_gather(out_weight, ('zh', 'zl', 'x', 'y'), axis=0, tiled=True)]
  transfers between devices with their start and end apart: 24 -> 25, of which waited for: 11 -> 13; matrix products, arithmetic and copies ran while one was open for 6% -> 5% of each run, Pallas kernels for 19% -> 12%
where the time goes in v1:
time: 153 us; the launch traced here: 152 us
  starting transfers between devices  58.4 us (38%)
  waiting for transfers between devices  37.4 us (24%)
  Pallas kernels  28.7 us (19%)
  between operations  13.5 us (9%)
  local copies, waits for them, and re-layouts  11.9 us (8%)
  other arithmetic  2.17 us (1%)
    ppermute x24, starting transfers between devices, shifted(): lax.ppermute(array, axis, [(i, (i + step) % size) for i in range(size)])  58.4 us
    ppermute x24, waiting for transfers between devices, shifted(): lax.ppermute(array, axis, [(i, (i + step) % size) for i in range(size)])  30 us
    pallas_call x2, Pallas kernels, project(): pl.pallas_call(project_kernel, out_shape=[jax.ShapeDtypeStruct((tok, 4 *...  15.4 us
    pallas_call x1, Pallas kernels, attention(): pl.pallas_call(functools.partial(attention_kernel, groups, sec, nsec), ou...  11.1 us
    all_gather x1, waiting for transfers between devices, per_device(): lax.all_gather(out_weight, ('zh', 'zl', 'x', 'y'), axis=0, tiled=True)  6.66 us
    unnamed x22, local copies, waits for them, and re-layouts  5.9 us
    dynamic_slice x2, local copies, waits for them, and re-layouts, head_slice(): return lax.dynamic_slice_in_dim(array[0], wrap(y + shift) * wide, wide, 1)  3.11 us
  transfers between devices with their start and end apart: 25, of which 13 were waited for; matrix products, arithmetic and copies ran while one was open for 5% of the time, Pallas kernels for 12%

profile of v1, /device:TPU:1, one launch (start us, length us, event | category | flops | bytes accessed | tf_op | source)
XLA Modules:
  0.0 152.1 jit_solution(10555380929445672084)
XLA Ops:
  8.4 3.8 %collective-permute-start.5 = (bf16[224,256]{1,0:T(8,128)(2,1)S(1)}, bf16[224,256]{1,0:T(8,128)(2,1)S(1)}, u32[]{:S(2)}, u32[]{:S(2)}) collective-permute-start(bf16[224,256]{1,0:T(8,128)(2,1)S(1)} %pad_maximum_fusion.3), channel_id=1, source_target_pairs={{0,2},{1,3},{2,0},{3,1},{4,6},{5,7},{6,4},{7,5},{8,10},{9,11},{10,... | collective-permute-start | bytes 344072 | tf_op jit(solution)/shard_map/ppermute | solution.py:20
  14.8 2.8 %collective-permute-done.4 = bf16[224,256]{1,0:T(8,128)(2,1)S(1)} collective-permute-done((bf16[224,256]{1,0:T(8,128)(2,1)S(1)}, bf16[224,256]{1,0:T(8,128)(2,1)S(1)}, u32[]{:S(2)}, u32[]{:S(2)}) %collective-permute-start.4) | collective-permute-done | bytes 114720 | tf_op jit(solution)/shard_map/ppermute | solution.py:20
  18.1 1.7 %collective-permute-start.10 = (bf16[4,224,256]{2,1,0:T(8,128)(2,1)S(1)}, bf16[4,224,256]{2,1,0:T(8,128)(2,1)S(1)}, u32[]{:S(2)}, u32[]{:S(2)}) collective-permute-start(bf16[4,224,256]{2,1,0:T(8,128)(2,1)S(1)} %pad_maximum_fusion.refs_4_), channel_id=1, source_target_pairs={{0,16},{16,0},{1,17},{17,1},{2,18},{18,2},{3,19},{19,3},{4,20},{20... | collective-permute-start | bytes 1376264 | tf_op jit(solution)/shard_map/ppermute | solution.py:20
  21.0 1.5 collective-permute-start.7
  22.5 6.5 %collective-permute-done.10.refs_9_ = bf16[4,224,256]{2,1,0:T(8,128)(2,1)S(1)} collective-permute-done((bf16[4,224,256]{2,1,0:T(8,128)(2,1)S(1)}, bf16[4,224,256]{2,1,0:T(8,128)(2,1)S(1)}, u32[]{:S(2)}, u32[]{:S(2)}) %collective-permute-start.10) | collective-permute-done | bytes 458784 | tf_op jit(solution)/shard_map/ppermute | solution.py:20
  31.7 2.0 %dynamic-slice_bitcast_fusion = (bf16[224,640]{1,0:T(8,128)(2,1)}, bf16[224,640]{1,0:T(8,128)(2,1)S(1)}, bf16[224,640]{1,0:T(8,128)(2,1)S(1)}, bf16[224,640]{1,0:T(8,128)(2,1)S(1)}) fusion(bf16[1,224,2560]{2,1,0:T(8,128)(2,1)} %param.7, s32[]{:T(128)S(6)} %select_n.31, s32[]{:T(128)S(6)} %select_n.29, s32[]{:T(128)S(6)} %select_n.28, s32[]{:T(128)S(6)} %select_n.30), kind=kLoop, calls=%fused_computation.1 | loop fusion | bytes 2293776 | tf_op jit(solution)/shard_map/dynamic_slice | solution.py:295
  33.7 2.8 %collective-permute-start = (bf16[224,640]{1,0:T(8,128)(2,1)S(1)}, bf16[224,640]{1,0:T(8,128)(2,1)S(1)}, u32[]{:S(2)}, u32[]{:S(2)}) collective-permute-start(bf16[224,640]{1,0:T(8,128)(2,1)S(1)} %get-tuple-element.24), channel_id=1, source_target_pairs={{0,1},{1,2},{2,3},{3,0},{4,5},{5,6},{6,7},{7,4},{8,9},{9,10},{10,1... | collective-permute-start | bytes 860168 | tf_op jit(solution)/shard_map/ppermute | solution.py:20
  36.5 1.5 %collective-permute-start.1 = (bf16[224,640]{1,0:T(8,128)(2,1)S(1)}, bf16[224,640]{1,0:T(8,128)(2,1)S(1)}, u32[]{:S(2)}, u32[]{:S(2)}) collective-permute-start(bf16[224,640]{1,0:T(8,128)(2,1)S(1)} %get-tuple-element.26), channel_id=1, source_target_pairs={{0,3},{1,0},{2,1},{3,2},{4,7},{5,4},{6,5},{7,6},{8,11},{9,8},{10,9... | collective-permute-start | bytes 860168 | tf_op jit(solution)/shard_map/ppermute | solution.py:20
  40.8 3.1 %collective-permute-done.11.refs_10_ = bf16[4,224,256]{2,1,0:T(8,128)(2,1)S(1)} collective-permute-done((bf16[4,224,256]{2,1,0:T(8,128)(2,1)S(1)}, bf16[4,224,256]{2,1,0:T(8,128)(2,1)S(1)}, u32[]{:S(2)}, u32[]{:S(2)}) %collective-permute-start.11) | collective-permute-done | bytes 458784 | tf_op jit(solution)/shard_map/ppermute | solution.py:20
  44.6 2.7 %collective-permute-start.9 = (bf16[2,224,256]{2,1,0:T(8,128)(2,1)}, bf16[2,224,256]{2,1,0:T(8,128)(2,1)}, u32[]{:S(2)}, u32[]{:S(2)}) collective-permute-start(bf16[2,224,256]{2,1,0:T(8,128)(2,1)} %slice.17), channel_id=1, source_target_pairs={{0,12},{4,0},{8,4},{12,8},{1,13},{5,1},{9,5},{13,9},{2,14},{6,2},{... | collective-permute-start | bytes 688136 | tf_op jit(solution)/shard_map/ppermute | solution.py:20
  49.4 2.7 %collective-permute-start.14 = (bf16[2,224,256]{2,1,0:T(8,128)(2,1)}, bf16[2,224,256]{2,1,0:T(8,128)(2,1)}, u32[]{:S(2)}, u32[]{:S(2)}) collective-permute-start(bf16[2,224,256]{2,1,0:T(8,128)(2,1)} %slice.19), channel_id=1, source_target_pairs={{0,12},{4,0},{8,4},{12,8},{1,13},{5,1},{9,5},{13,9},{2,14},{6,2},{... | collective-permute-start | bytes 688136 | tf_op jit(solution)/shard_map/ppermute | solution.py:20
  55.3 8.9 %collective-permute-done.13.refs_12_ = bf16[2,224,256]{2,1,0:T(8,128)(2,1)} collective-permute-done((bf16[2,224,256]{2,1,0:T(8,128)(2,1)}, bf16[2,224,256]{2,1,0:T(8,128)(2,1)}, u32[]{:S(2)}, u32[]{:S(2)}) %collective-permute-start.13) | collective-permute-done | bytes 229408 | tf_op jit(solution)/shard_map/ppermute | solution.py:20
  68.0 11.1 %attend.1 = (bf16[224,640]{1,0:T(8,128)(2,1)S(1)}, bf16[224,640]{1,0:T(8,128)(2,1)S(1)}, bf16[224,640]{1,0:T(8,128)(2,1)S(1)}, bf16[224,640]{1,0:T(8,128)(2,1)S(1)}) custom-call(s32[3]{0:T(128)S(1)} %pad_add_fusion.coords, s32[64]{0:T(128)S(1)} %copy-done.6, s32[64]{0:T(128)S(1)} %bitcast.37, s32[2]{0:T(128)S(1)} %pad_add_fusion.1.starts, ...), custom_call_target="tpu_custom_call" | custom-call | flops 8000000000 | bytes 6000000 | tf_op jit(solution)/shard_map/attend/pallas_call | solution.py:178
  79.0 2.6 %collective-permute-start.15 = (bf16[224,640]{1,0:T(8,128)(2,1)S(1)}, bf16[224,640]{1,0:T(8,128)(2,1)S(1)}, u32[]{:S(2)}, u32[]{:S(2)}) collective-permute-start(bf16[224,640]{1,0:T(8,128)(2,1)S(1)} %get-tuple-element.14), channel_id=1, source_target_pairs={{0,1},{1,2},{2,3},{3,0},{4,5},{5,6},{6,7},{7,4},{8,9},{9,10},{10,1... | collective-permute-start | bytes 860168 | tf_op jit(solution)/shard_map/ppermute | solution.py:20
  81.7 1.8 %collective-permute-start.16 = (bf16[224,640]{1,0:T(8,128)(2,1)S(1)}, bf16[224,640]{1,0:T(8,128)(2,1)S(1)}, u32[]{:S(2)}, u32[]{:S(2)}) collective-permute-start(bf16[224,640]{1,0:T(8,128)(2,1)S(1)} %get-tuple-element.15), channel_id=1, source_target_pairs={{0,3},{1,0},{2,1},{3,2},{4,7},{5,4},{6,5},{7,6},{8,11},{9,8},{10,9... | collective-permute-start | bytes 860168 | tf_op jit(solution)/shard_map/ppermute | solution.py:20
  84.6 8.8 %collective-permute-start.18 = (bf16[224,640]{1,0:T(8,128)(2,1)S(1)}, bf16[224,640]{1,0:T(8,128)(2,1)S(1)}, u32[]{:S(2)}, u32[]{:S(2)}) collective-permute-start(bf16[224,640]{1,0:T(8,128)(2,1)S(1)} %get-tuple-element.13.refs_0_), channel_id=1, source_target_pairs={{0,32},{32,0},{1,33},{33,1},{2,34},{34,2},{3,35},{35,3},{4,36},{36... | collective-permute-start | bytes 860168 | tf_op jit(solution)/shard_map/ppermute | solution.py:20
  94.3 10.5 %collective-permute-start.19 = (bf16[224,640]{1,0:T(8,128)(2,1)S(1)}, bf16[224,640]{1,0:T(8,128)(2,1)S(1)}, u32[]{:S(2)}, u32[]{:S(2)}) collective-permute-start(bf16[224,640]{1,0:T(8,128)(2,1)S(1)} %collective-permute-done.15.refs_1_), channel_id=1, source_target_pairs={{0,32},{32,0},{1,33},{33,1},{2,34},{34,2},{3,35},{35,3},{4,36},{36... | collective-permute-start | bytes 860168 | tf_op jit(solution)/shard_map/ppermute | solution.py:20
  105.7 1.9 %collective-permute-done.17.refs_3_ = bf16[224,640]{1,0:T(8,128)(2,1)S(1)} collective-permute-done((bf16[224,640]{1,0:T(8,128)(2,1)S(1)}, bf16[224,640]{1,0:T(8,128)(2,1)S(1)}, u32[]{:S(2)}, u32[]{:S(2)}) %collective-permute-start.17) | collective-permute-done | bytes 286752 | tf_op jit(solution)/shard_map/ppermute | solution.py:20
  107.6 8.6 %collective-permute-start.21 = (bf16[224,640]{1,0:T(8,128)(2,1)S(1)}, bf16[224,640]{1,0:T(8,128)(2,1)S(1)}, u32[]{:S(2)}, u32[]{:S(2)}) collective-permute-start(bf16[224,640]{1,0:T(8,128)(2,1)S(1)} %collective-permute-done.17.refs_3_), channel_id=1, source_target_pairs={{0,32},{32,0},{1,33},{33,1},{2,34},{34,2},{3,35},{35,3},{4,36},{36... | collective-permute-start | bytes 860168 | tf_op jit(solution)/shard_map/ppermute | solution.py:20
  117.4 6.7 %all-gather.2.cloned.1.call-done.refs_8_ = bf16[5120,1280]{1,0:T(8,128)(2,1)} async-done(((bf16[80,1280]{1,0:T(8,128)(2,1)}), bf16[5120,1280]{1,0:T(8,128)(2,1)}) %all-gather.2.cloned.1.call-update) | async-done | bytes 13107216 | tf_op jit(solution)/shard_map/all_gather | solution.py:309
  124.0 7.7 %project.2 = (bf16[224,5120]{1,0:T(8,128)(2,1)}, bf16[224,1280]{1,0:T(8,128)(2,1)S(1)}) custom-call(s32[3]{0:T(128)S(1)} %pad_add_fusion.coords, s32[1]{0:T(128)} %bitcast.core, bf16[224,640]{1,0:T(8,128)(2,1)S(1)} %get-tuple-element.13.refs_0_, bf16[224,640]{1,0:T(8,128)(2,1)S(1)} %collective-permute-done.15.refs_1_, ...), custom_call_target="tpu_custom_call" | custom-call | flops 3000000000 | bytes 9000000 | tf_op jit(solution)/shard_map/project/pallas_call | solution.py:225
  132.4 7.7 %project.3 = (bf16[224,5120]{1,0:T(8,128)(2,1)}, bf16[224,1280]{1,0:T(8,128)(2,1)S(1)}) custom-call(s32[3]{0:T(128)S(1)} %pad_add_fusion.coords, s32[1]{0:T(128)} %bitcast.core, bf16[224,640]{1,0:T(8,128)(2,1)S(1)} %get-tuple-element.13.refs_0_, bf16[224,640]{1,0:T(8,128)(2,1)S(1)} %collective-permute-done.15.refs_1_, ...), custom_call_target="tpu_custom_call", output_to_operand_aliasing={{0}: (11, {})} | custom-call | flops 3000000000 | bytes 9000000 | tf_op jit(solution)/shard_map/project/pallas_call | solution.py:225
  140.1 2.0 %collective-permute-done.23.second = bf16[224,1280]{1,0:T(8,128)(2,1)S(1)} collective-permute-done((bf16[224,1280]{1,0:T(8,128)(2,1)S(1)}, bf16[224,1280]{1,0:T(8,128)(2,1)S(1)}, u32[]{:S(2)}, u32[]{:S(2)}) %collective-permute-start.23) | collective-permute-done | bytes 573472 | tf_op jit(solution)/shard_map/ppermute | solution.py:20
  142.9 2.3 %merge.1 = bf16[224,5120]{1,0:T(8,128)(2,1)} custom-call(s32[1]{0:T(128)} %bitcast.core, bf16[224,1280]{1,0:T(8,128)(2,1)} %copy-done.8, bf16[224,1280]{1,0:T(8,128)(2,1)} %copy-done.9, bf16[224,5120]{1,0:T(8,128)(2,1)} %get-tuple-element.20.whole), custom_call_target="tpu_custom_call", output_to_operand_aliasing={{}: (3, {})} | custom-call | bytes 3000000 | tf_op jit(solution)/shard_map/merge/pallas_call | solution.py:268
  (67 shorter events, 27.0 us)
Async XLA Ops:
  6.5 117.5 %all-gather.2.cloned.1.call-start = ((), (), s32[]{:S(2)}) async-start(), calls=%async_computation | async-start | bytes 13312000 | tf_op jit(solution)/shard_map/all_gather | solution.py:309
  8.4 6.4 %collective-permute-start.5 = (bf16[224,256]{1,0:T(8,128)(2,1)S(1)}, bf16[224,256]{1,0:T(8,128)(2,1)S(1)}, u32[]{:S(2)}, u32[]{:S(2)}) collective-permute-start(bf16[224,256]{1,0:T(8,128)(2,1)S(1)} %pad_maximum_fusion.3), channel_id=1, source_target_pairs={{0,2},{1,3},{2,0},{3,1},{4,6},{5,7},{6,4},{7,5},{8,10},{9,11},{10,... | collective-permute-start | bytes 344072 | tf_op jit(solution)/shard_map/ppermute | solution.py:20
  12.2 5.4 %collective-permute-start.4 = (bf16[224,256]{1,0:T(8,128)(2,1)S(1)}, bf16[224,256]{1,0:T(8,128)(2,1)S(1)}, u32[]{:S(2)}, u32[]{:S(2)}) collective-permute-start(bf16[224,256]{1,0:T(8,128)(2,1)S(1)} %pad_maximum_fusion.2), channel_id=1, source_target_pairs={{0,3},{1,0},{2,1},{3,2},{4,7},{5,4},{6,5},{7,6},{8,11},{9,8},{10,9... | collective-permute-start | bytes 344072 | tf_op jit(solution)/shard_map/ppermute | solution.py:20
  13.1 4.9 %collective-permute-start.3 = (bf16[224,256]{1,0:T(8,128)(2,1)S(1)}, bf16[224,256]{1,0:T(8,128)(2,1)S(1)}, u32[]{:S(2)}, u32[]{:S(2)}) collective-permute-start(bf16[224,256]{1,0:T(8,128)(2,1)S(1)} %pad_maximum_fusion.1), channel_id=1, source_target_pairs={{0,1},{1,2},{2,3},{3,0},{4,5},{5,6},{6,7},{7,4},{8,9},{9,10},{10,1... | collective-permute-start | bytes 344072 | tf_op jit(solution)/shard_map/ppermute | solution.py:20
  18.1 10.9 %collective-permute-start.10 = (bf16[4,224,256]{2,1,0:T(8,128)(2,1)S(1)}, bf16[4,224,256]{2,1,0:T(8,128)(2,1)S(1)}, u32[]{:S(2)}, u32[]{:S(2)}) collective-permute-start(bf16[4,224,256]{2,1,0:T(8,128)(2,1)S(1)} %pad_maximum_fusion.refs_4_), channel_id=1, source_target_pairs={{0,16},{16,0},{1,17},{17,1},{2,18},{18,2},{3,19},{19,3},{4,20},{20... | collective-permute-start | bytes 1376264 | tf_op jit(solution)/shard_map/ppermute | solution.py:20
  19.8 16.7 %collective-permute-start.6 = (bf16[4,224,256]{2,1,0:T(8,128)(2,1)S(1)}, bf16[4,224,256]{2,1,0:T(8,128)(2,1)S(1)}, u32[]{:S(2)}, u32[]{:S(2)}) collective-permute-start(bf16[4,224,256]{2,1,0:T(8,128)(2,1)S(1)} %pad_maximum_fusion.refs_4_), channel_id=1, source_target_pairs={{0,4},{4,8},{8,12},{12,0},{1,5},{5,9},{9,13},{13,1},{2,6},{6,10},{... | collective-permute-start | bytes 1376264 | tf_op jit(solution)/shard_map/ppermute | solution.py:20
  21.0 17.7 %collective-permute-start.7 = (bf16[4,224,256]{2,1,0:T(8,128)(2,1)S(1)}, bf16[4,224,256]{2,1,0:T(8,128)(2,1)S(1)}, u32[]{:S(2)}, u32[]{:S(2)}) collective-permute-start(bf16[4,224,256]{2,1,0:T(8,128)(2,1)S(1)} %pad_maximum_fusion.refs_4_), channel_id=1, source_target_pairs={{0,12},{4,0},{8,4},{12,8},{1,13},{5,1},{9,5},{13,9},{2,14},{6,2},{... | collective-permute-start | bytes 1376264 | tf_op jit(solution)/shard_map/ppermute | solution.py:20
  29.0 14.9 %collective-permute-start.11 = (bf16[4,224,256]{2,1,0:T(8,128)(2,1)S(1)}, bf16[4,224,256]{2,1,0:T(8,128)(2,1)S(1)}, u32[]{:S(2)}, u32[]{:S(2)}) collective-permute-start(bf16[4,224,256]{2,1,0:T(8,128)(2,1)S(1)} %collective-permute-done.10.refs_9_), channel_id=1, source_target_pairs={{0,4},{4,8},{8,12},{12,0},{1,5},{5,9},{9,13},{13,1},{2,6},{6,10},{... | collective-permute-start | bytes 1376264 | tf_op jit(solution)/shard_map/ppermute | solution.py:20
  30.2 14.4 %collective-permute-start.12 = (bf16[4,224,256]{2,1,0:T(8,128)(2,1)S(1)}, bf16[4,224,256]{2,1,0:T(8,128)(2,1)S(1)}, u32[]{:S(2)}, u32[]{:S(2)}) collective-permute-start(bf16[4,224,256]{2,1,0:T(8,128)(2,1)S(1)} %collective-permute-done.10.refs_9_), channel_id=1, source_target_pairs={{0,12},{4,0},{8,4},{12,8},{1,13},{5,1},{9,5},{13,9},{2,14},{6,2},{... | collective-permute-start | bytes 1376264 | tf_op jit(solution)/shard_map/ppermute | solution.py:20
  33.7 14.3 %collective-permute-start = (bf16[224,640]{1,0:T(8,128)(2,1)S(1)}, bf16[224,640]{1,0:T(8,128)(2,1)S(1)}, u32[]{:S(2)}, u32[]{:S(2)}) collective-permute-start(bf16[224,640]{1,0:T(8,128)(2,1)S(1)} %get-tuple-element.24), channel_id=1, source_target_pairs={{0,1},{1,2},{2,3},{3,0},{4,5},{5,6},{6,7},{7,4},{8,9},{9,10},{10,1... | collective-permute-start | bytes 860168 | tf_op jit(solution)/shard_map/ppermute | solution.py:20
  36.5 12.2 %collective-permute-start.1 = (bf16[224,640]{1,0:T(8,128)(2,1)S(1)}, bf16[224,640]{1,0:T(8,128)(2,1)S(1)}, u32[]{:S(2)}, u32[]{:S(2)}) collective-permute-start(bf16[224,640]{1,0:T(8,128)(2,1)S(1)} %get-tuple-element.26), channel_id=1, source_target_pairs={{0,3},{1,0},{2,1},{3,2},{4,7},{5,4},{6,5},{7,6},{8,11},{9,8},{10,9... | collective-permute-start | bytes 860168 | tf_op jit(solution)/shard_map/ppermute | solution.py:20
  38.8 15.4 %collective-permute-start.2 = (bf16[224,640]{1,0:T(8,128)(2,1)}, bf16[224,640]{1,0:T(8,128)(2,1)S(1)}, u32[]{:S(2)}, u32[]{:S(2)}) collective-permute-start(bf16[224,640]{1,0:T(8,128)(2,1)} %get-tuple-element.23), channel_id=1, source_target_pairs={{0,2},{1,3},{2,0},{3,1},{4,6},{5,7},{6,4},{7,5},{8,10},{9,11},{10,... | collective-permute-start | bytes 860168 | tf_op jit(solution)/shard_map/ppermute | solution.py:20
  43.9 11.0 %collective-permute-start.8 = (bf16[2,224,256]{2,1,0:T(8,128)(2,1)}, bf16[2,224,256]{2,1,0:T(8,128)(2,1)}, u32[]{:S(2)}, u32[]{:S(2)}) collective-permute-start(bf16[2,224,256]{2,1,0:T(8,128)(2,1)} %slice.16), channel_id=1, source_target_pairs={{0,4},{4,8},{8,12},{12,0},{1,5},{5,9},{9,13},{13,1},{2,6},{6,10},{... | collective-permute-start | bytes 688136 | tf_op jit(solution)/shard_map/ppermute | solution.py:20
  44.6 10.7 %collective-permute-start.9 = (bf16[2,224,256]{2,1,0:T(8,128)(2,1)}, bf16[2,224,256]{2,1,0:T(8,128)(2,1)}, u32[]{:S(2)}, u32[]{:S(2)}) collective-permute-start(bf16[2,224,256]{2,1,0:T(8,128)(2,1)} %slice.17), channel_id=1, source_target_pairs={{0,12},{4,0},{8,4},{12,8},{1,13},{5,1},{9,5},{13,9},{2,14},{6,2},{... | collective-permute-start | bytes 688136 | tf_op jit(solution)/shard_map/ppermute | solution.py:20
  48.7 15.5 %collective-permute-start.13 = (bf16[2,224,256]{2,1,0:T(8,128)(2,1)}, bf16[2,224,256]{2,1,0:T(8,128)(2,1)}, u32[]{:S(2)}, u32[]{:S(2)}) collective-permute-start(bf16[2,224,256]{2,1,0:T(8,128)(2,1)} %slice.18), channel_id=1, source_target_pairs={{0,4},{4,8},{8,12},{12,0},{1,5},{5,9},{9,13},{13,1},{2,6},{6,10},{... | collective-permute-start | bytes 688136 | tf_op jit(solution)/shard_map/ppermute | solution.py:20
  49.4 15.6 %collective-permute-start.14 = (bf16[2,224,256]{2,1,0:T(8,128)(2,1)}, bf16[2,224,256]{2,1,0:T(8,128)(2,1)}, u32[]{:S(2)}, u32[]{:S(2)}) collective-permute-start(bf16[2,224,256]{2,1,0:T(8,128)(2,1)} %slice.19), channel_id=1, source_target_pairs={{0,12},{4,0},{8,4},{12,8},{1,13},{5,1},{9,5},{13,9},{2,14},{6,2},{... | collective-permute-start | bytes 688136 | tf_op jit(solution)/shard_map/ppermute | solution.py:20
  79.0 15.3 %collective-permute-start.15 = (bf16[224,640]{1,0:T(8,128)(2,1)S(1)}, bf16[224,640]{1,0:T(8,128)(2,1)S(1)}, u32[]{:S(2)}, u32[]{:S(2)}) collective-permute-start(bf16[224,640]{1,0:T(8,128)(2,1)S(1)} %get-tuple-element.14), channel_id=1, source_target_pairs={{0,1},{1,2},{2,3},{3,0},{4,5},{5,6},{6,7},{7,4},{8,9},{9,10},{10,1... | collective-permute-start | bytes 860168 | tf_op jit(solution)/shard_map/ppermute | solution.py:20
  81.7 23.1 %collective-permute-start.16 = (bf16[224,640]{1,0:T(8,128)(2,1)S(1)}, bf16[224,640]{1,0:T(8,128)(2,1)S(1)}, u32[]{:S(2)}, u32[]{:S(2)}) collective-permute-start(bf16[224,640]{1,0:T(8,128)(2,1)S(1)} %get-tuple-element.15), channel_id=1, source_target_pairs={{0,3},{1,0},{2,1},{3,2},{4,7},{5,4},{6,5},{7,6},{8,11},{9,8},{10,9... | collective-permute-start | bytes 860168 | tf_op jit(solution)/shard_map/ppermute | solution.py:20
  83.5 24.2 %collective-permute-start.17 = (bf16[224,640]{1,0:T(8,128)(2,1)S(1)}, bf16[224,640]{1,0:T(8,128)(2,1)S(1)}, u32[]{:S(2)}, u32[]{:S(2)}) collective-permute-start(bf16[224,640]{1,0:T(8,128)(2,1)S(1)} %get-tuple-element.16), channel_id=1, source_target_pairs={{0,2},{1,3},{2,0},{3,1},{4,6},{5,7},{6,4},{7,5},{8,10},{9,11},{10,... | collective-permute-start | bytes 860168 | tf_op jit(solution)/shard_map/ppermute | solution.py:20
  84.6 31.6 %collective-permute-start.18 = (bf16[224,640]{1,0:T(8,128)(2,1)S(1)}, bf16[224,640]{1,0:T(8,128)(2,1)S(1)}, u32[]{:S(2)}, u32[]{:S(2)}) collective-permute-start(bf16[224,640]{1,0:T(8,128)(2,1)S(1)} %get-tuple-element.13.refs_0_), channel_id=1, source_target_pairs={{0,32},{32,0},{1,33},{33,1},{2,34},{34,2},{3,35},{35,3},{4,36},{36... | collective-permute-start | bytes 860168 | tf_op jit(solution)/shard_map/ppermute | solution.py:20
  94.3 21.9 %collective-permute-start.19 = (bf16[224,640]{1,0:T(8,128)(2,1)S(1)}, bf16[224,640]{1,0:T(8,128)(2,1)S(1)}, u32[]{:S(2)}, u32[]{:S(2)}) collective-permute-start(bf16[224,640]{1,0:T(8,128)(2,1)S(1)} %collective-permute-done.15.refs_1_), channel_id=1, source_target_pairs={{0,32},{32,0},{1,33},{33,1},{2,34},{34,2},{3,35},{35,3},{4,36},{36... | collective-permute-start | bytes 860168 | tf_op jit(solution)/shard_map/ppermute | solution.py:20
  104.8 11.4 %collective-permute-start.20 = (bf16[224,640]{1,0:T(8,128)(2,1)S(1)}, bf16[224,640]{1,0:T(8,128)(2,1)S(1)}, u32[]{:S(2)}, u32[]{:S(2)}) collective-permute-start(bf16[224,640]{1,0:T(8,128)(2,1)S(1)} %collective-permute-done.16.refs_2_), channel_id=1, source_target_pairs={{0,32},{32,0},{1,33},{33,1},{2,34},{34,2},{3,35},{35,3},{4,36},{36... | collective-permute-start | bytes 860168 | tf_op jit(solution)/shard_map/ppermute | solution.py:20
  107.6 9.8 %collective-permute-start.21 = (bf16[224,640]{1,0:T(8,128)(2,1)S(1)}, bf16[224,640]{1,0:T(8,128)(2,1)S(1)}, u32[]{:S(2)}, u32[]{:S(2)}) collective-permute-start(bf16[224,640]{1,0:T(8,128)(2,1)S(1)} %collective-permute-done.17.refs_3_), channel_id=1, source_target_pairs={{0,32},{32,0},{1,33},{33,1},{2,34},{34,2},{3,35},{35,3},{4,36},{36... | collective-permute-start | bytes 860168 | tf_op jit(solution)/shard_map/ppermute | solution.py:20
  131.7 8.4 %collective-permute-start.22 = (bf16[224,1280]{1,0:T(8,128)(2,1)S(1)}, bf16[224,1280]{1,0:T(8,128)(2,1)S(1)}, u32[]{:S(2)}, u32[]{:S(2)}) collective-permute-start(bf16[224,1280]{1,0:T(8,128)(2,1)S(1)} %get-tuple-element.17), channel_id=1, source_target_pairs={{0,32},{32,0},{1,33},{33,1},{2,34},{34,2},{3,35},{35,3},{4,36},{36... | collective-permute-start | bytes 1720328 | tf_op jit(solution)/shard_map/ppermute | solution.py:20
  (12 other events, 137.8 us)
Sparse Core Ops, SparseCore 0:
  10.2 113.7 all-gather.1

commit v2 on v1

--- a/solution.py
+++ b/solution.py
@@ -13,6 +13,7 @@
 SHIFTS = (0, -1, 1, 2)
 BLOCK_KEYS = 2048
 TAIL_STEP = 256
+LOADS = 5
 ROW_TILE = 16
 
 
@@ -198,87 +199,103 @@
 
 def project_kernel(coords, core, *refs):
     att_refs, weights = refs[:8], refs[8]
-    own_out, other_out, att = refs[-3:]
+    whole, other_out, att, held, own, sems = refs[9:]
     tok, wide = att_refs[0].shape
-
-    @pl.when(pl.program_id(0) == 0)
-    def _():
-        for who in range(2):
-            for j in range(4):
-                head = wrap(coords[2] + SHIFTS[j])
-                at = pl.multiple_of(head * wide, HD)
-                att[pl.ds(who * tok, tok), pl.ds(at, wide)] = att_refs[4 * who + j][...]
-
-    got = jnp.dot(att[...], weights[...], preferred_element_type=jnp.float32)
-    got = got.astype(own_out.dtype)
-    own_out[...] = got[:tok]
-    other_out[...] = got[tok:]
-
-
-def project(coords, core, own_att, other_att, weights, cols, half, whole):
+    cols = weights.shape[1]
+    rows = RING * wide
+    piece = rows // LOADS
+
+    def loads(half):
+        for i in range(LOADS):
+            at = pl.ds(half * rows + i * piece, piece)
+            yield pltpu.make_async_copy(weights.at[at, :], held.at[at, :], sems.at[half])
+
+    def store(half):
+        at = pl.multiple_of((half * 2 + core[0]) * cols, HD)
+        return pltpu.make_async_copy(own.at[half], whole.at[:, pl.ds(at, cols)], sems.at[2 + half])
+
+    for half in range(2):
+        for load in loads(half):
+            load.start()
+    for who in range(2):
+        for j in range(4):
+            head = wrap(coords[2] + SHIFTS[j])
+            at = pl.multiple_of(head * wide, HD)
+            att[pl.ds(who * tok, tok), pl.ds(at, wide)] = att_refs[4 * who + j][...]
+    for half in range(2):
+        for load in loads(half):
+            load.wait()
+        for first in range(0, cols, 2 * HD):
+            got = jnp.dot(
+                att[...],
+                held[pl.ds(half * rows, rows), pl.ds(first, 2 * HD)],
+                preferred_element_type=jnp.float32,
+            ).astype(own.dtype)
+            own[half, :, pl.ds(first, 2 * HD)] = got[:tok]
+            other_out[half, :, pl.ds(first, 2 * HD)] = got[tok:]
+        store(half).start()
+    for half in range(2):
+        store(half).wait()
+
+
+def project(coords, core, own_att, other_att, weights):
     tok, wide = own_att[0].shape
-    rows = RING * wide
-    step = 2 * HD
-    steps = cols // step
-    piece = pl.BlockSpec((tok, wide), lambda i, *_: (0, 0))
-    given = [] if whole is None else [whole]
+    rows, cols = RING * wide, weights.shape[1]
+    smem = pl.BlockSpec(memory_space=pltpu.SMEM)
+    vmem = pl.BlockSpec(memory_space=pltpu.VMEM)
+    anywhere = pl.BlockSpec(memory_space=pl.ANY)
     return pl.pallas_call(
         project_kernel,
         out_shape=[
             jax.ShapeDtypeStruct((tok, 4 * cols), jnp.bfloat16),
-            jax.ShapeDtypeStruct((tok, cols), jnp.bfloat16),
+            jax.ShapeDtypeStruct((2, tok, cols), jnp.bfloat16),
         ],
-        grid_spec=pltpu.PrefetchScalarGridSpec(
-            num_scalar_prefetch=2,
-            grid=(steps,),
-            in_specs=[piece] * 8
-            + [pl.BlockSpec((rows, step), lambda i, *_: (half, i))]
-            + [pl.BlockSpec(memory_space=pl.ANY)] * len(given),
-            out_specs=[
-                pl.BlockSpec(
-                    (tok, step), lambda i, where, core: (0, (half * 2 + core[0]) * steps + i)
-                ),
-                pl.BlockSpec((tok, step), lambda i, *_: (0, i)),
-            ],
-            scratch_shapes=[pltpu.VMEM((2 * tok, rows), jnp.bfloat16)],
-        ),
-        input_output_aliases={11: 0} if given else {},
+        in_specs=[smem] * 2 + [vmem] * 8 + [anywhere],
+        out_specs=[anywhere, vmem],
+        scratch_shapes=[
+            pltpu.VMEM((2 * tok, rows), jnp.bfloat16),
+            pltpu.VMEM((2 * rows, cols), jnp.bfloat16),
+            pltpu.VMEM((2, tok, cols), jnp.bfloat16),
+            pltpu.SemaphoreType.DMA((4,)),
+        ],
         compiler_params=pltpu.CompilerParams(vmem_limit_bytes=48 * 2**20),
         cost_estimate=pl.CostEstimate(
-            flops=3 * 10**9, bytes_accessed=9 * 10**6, transcendentals=0
+            flops=6 * 10**9, bytes_accessed=18 * 10**6, transcendentals=0
         ),
         name="project",
-    )(coords, core, *own_att, *other_att, weights, *given)
-
-
-def merge_kernel(core, first, second, whole, out):
-    del core, whole
-
-    @pl.when(pl.program_id(0) == 0)
-    def _():
-        out[...] = first[...]
-
-    @pl.when(pl.program_id(0) == 1)
-    def _():
-        out[...] = second[...]
+    )(coords, core, *own_att, *other_att, weights)
+
+
+def merge_kernel(core, theirs, whole, out, sems):
+    del whole
+    cols = theirs.shape[2]
+
+    def store(half):
+        at = pl.multiple_of((half * 2 + 1 - core[0]) * cols, HD)
+        return pltpu.make_async_copy(theirs.at[half], out.at[:, pl.ds(at, cols)], sems.at[half])
+
+    for half in range(2):
+        store(half).start()
+    for half in range(2):
+        store(half).wait()
 
 
 def merge(core, theirs, whole):
-    tok, cols = theirs[0].shape
+    anywhere = pl.BlockSpec(memory_space=pl.ANY)
     return pl.pallas_call(
         merge_kernel,
         out_shape=jax.ShapeDtypeStruct(whole.shape, whole.dtype),
-        grid_spec=pltpu.PrefetchScalarGridSpec(
-            num_scalar_prefetch=1,
-            grid=(2,),
-            in_specs=[pl.BlockSpec((tok, cols), lambda i, core: (0, 0))] * 2
-            + [pl.BlockSpec(memory_space=pl.ANY)],
-            out_specs=pl.BlockSpec((tok, cols), lambda i, core: (0, i * 2 + 1 - core[0])),
-        ),
-        input_output_aliases={3: 0},
+        in_specs=[
+            pl.BlockSpec(memory_space=pltpu.SMEM),
+            pl.BlockSpec(memory_space=pltpu.VMEM),
+            anywhere,
+        ],
+        out_specs=anywhere,
+        scratch_shapes=[pltpu.SemaphoreType.DMA((2,))],
+        input_output_aliases={2: 0},
         cost_estimate=pl.CostEstimate(flops=0, bytes_accessed=3 * 10**6, transcendentals=0),
         name="merge",
-    )(core, *theirs, whole)
+    )(core, theirs, whole)
 
 
 def per_device(query, keys, values, section_order, kept_sections, segment_ids, out_weight):
@@ -305,7 +322,6 @@
     far = shifted(near, "zl", 1, 2)
     kv_all = ring_gather(near)("x") + ring_gather(far)("x")
 
-    cols = out_weight.shape[1]
     weights = lax.all_gather(out_weight, ("zh", "zl", "x", "y"), axis=0, tiled=True)
 
     attended = attention(
@@ -318,13 +334,8 @@
     own_att = [back[s] for s in SHIFTS]
     other_att = [shifted(a, "c", 1, 2) for a in own_att]
     which = core[None].astype(jnp.int32)
-    whole, theirs = None, []
-    for half in range(2):
-        whole, for_other = project(
-            coords, which, own_att, other_att, weights, cols, half, whole
-        )
-        theirs.append(shifted(for_other, "c", 1, 2))
-    return merge(which, theirs, whole)[None]
+    whole, for_other = project(coords, which, own_att, other_att, weights)
+    return merge(which, shifted(for_other, "c", 1, 2), whole)[None]
 
 
 def wrap_static(shift):

time: 153 us -> 150 us (0.980)
  local copies, waits for them, and re-layouts: 11.9 us -> 8.61 us
  Pallas kernels: 28.7 us -> 25.8 us
  waiting for transfers between devices: 37.4 us -> 40.2 us
    pallas_call x2 -> x1, Pallas kernels: 15.4 us -> 12.1 us  [project(): pl.pallas_call(project_kernel, out_shape=[jax.ShapeDtypeStruct((tok, 4 *...]
    unnamed x22 -> x12, local copies, waits for them, and re-layouts: 5.9 us -> 2.67 us
    ppermute x24 -> x23, waiting for transfers between devices: 30 us -> 32.9 us  [shifted(): lax.ppermute(array, axis, [(i, (i + step) % size) for i in range(size)])]
    ppermute x24 -> x23, starting transfers between devices: 58.4 us -> 59 us  [shifted(): lax.ppermute(array, axis, [(i, (i + step) % size) for i in range(size)])]
  transfers between devices with their start and end apart: 25 -> 24, of which waited for: 13 -> 9; matrix products, arithmetic and copies ran while one was open for 5% -> 5% of each run, Pallas kernels for 12% -> 8%
where the time goes in v2:
time: 150 us; the launch traced here: 149 us
  starting transfers between devices  59 us (39%)
  waiting for transfers between devices  40.2 us (27%)
  Pallas kernels  25.8 us (17%)
  between operations  13.6 us (9%)
  local copies, waits for them, and re-layouts  8.61 us (6%)
  other arithmetic  2.27 us (2%)
    ppermute x23, starting transfers between devices, shifted(): lax.ppermute(array, axis, [(i, (i + step) % size) for i in range(size)])  59 us
    ppermute x23, waiting for transfers between devices, shifted(): lax.ppermute(array, axis, [(i, (i + step) % size) for i in range(size)])  32.9 us
    pallas_call x1, Pallas kernels, project(): pl.pallas_call(project_kernel, out_shape=[jax.ShapeDtypeStruct((tok, 4 *...  12.1 us
    pallas_call x1, Pallas kernels, attention(): pl.pallas_call(functools.partial(attention_kernel, groups, sec, nsec), ou...  11.4 us
    all_gather x1, waiting for transfers between devices, per_device(): lax.all_gather(out_weight, ('zh', 'zl', 'x', 'y'), axis=0, tiled=True)  6.57 us
    dynamic_slice x2, local copies, waits for them, and re-layouts, head_slice(): return lax.dynamic_slice_in_dim(array[0], wrap(y + shift) * wide, wide, 1)  3.11 us
  transfers between devices with their start and end apart: 24, of which 9 were waited for; matrix products, arithmetic and copies ran while one was open for 5% of the time, Pallas kernels for 8%

profile of v2, /device:TPU:1, one launch (start us, length us, event | category | flops | bytes accessed | tf_op | source)
XLA Modules:
  0.0 149.4 jit_solution(12337622559205286640)
XLA Ops:
  8.4 2.2 %collective-permute-start.3 = (bf16[224,256]{1,0:T(8,128)(2,1)S(1)}, bf16[224,256]{1,0:T(8,128)(2,1)S(1)}, u32[]{:S(2)}, u32[]{:S(2)}) collective-permute-start(bf16[224,256]{1,0:T(8,128)(2,1)S(1)} %pad_maximum_fusion.1), channel_id=1, source_target_pairs={{0,1},{1,2},{2,3},{3,0},{4,5},{5,6},{6,7},{7,4},{8,9},{9,10},{10,1... | collective-permute-start | bytes 344072 | tf_op jit(solution)/shard_map/ppermute | solution.py:21
  10.6 1.5 %collective-permute-start.4 = (bf16[224,256]{1,0:T(8,128)(2,1)S(1)}, bf16[224,256]{1,0:T(8,128)(2,1)S(1)}, u32[]{:S(2)}, u32[]{:S(2)}) collective-permute-start(bf16[224,256]{1,0:T(8,128)(2,1)S(1)} %pad_maximum_fusion.2), channel_id=1, source_target_pairs={{0,3},{1,0},{2,1},{3,2},{4,7},{5,4},{6,5},{7,6},{8,11},{9,8},{10,9... | collective-permute-start | bytes 344072 | tf_op jit(solution)/shard_map/ppermute | solution.py:21
  12.1 1.7 %collective-permute-start.5 = (bf16[224,256]{1,0:T(8,128)(2,1)S(1)}, bf16[224,256]{1,0:T(8,128)(2,1)S(1)}, u32[]{:S(2)}, u32[]{:S(2)}) collective-permute-start(bf16[224,256]{1,0:T(8,128)(2,1)S(1)} %pad_maximum_fusion.3), channel_id=1, source_target_pairs={{0,2},{1,3},{2,0},{3,1},{4,6},{5,7},{6,4},{7,5},{8,10},{9,11},{10,... | collective-permute-start | bytes 344072 | tf_op jit(solution)/shard_map/ppermute | solution.py:21
  14.7 3.5 %collective-permute-done.5 = bf16[224,256]{1,0:T(8,128)(2,1)S(1)} collective-permute-done((bf16[224,256]{1,0:T(8,128)(2,1)S(1)}, bf16[224,256]{1,0:T(8,128)(2,1)S(1)}, u32[]{:S(2)}, u32[]{:S(2)}) %collective-permute-start.5) | collective-permute-done | bytes 114720 | tf_op jit(solution)/shard_map/ppermute | solution.py:21
  18.3 1.6 %collective-permute-start.10 = (bf16[4,224,256]{2,1,0:T(8,128)(2,1)S(1)}, bf16[4,224,256]{2,1,0:T(8,128)(2,1)S(1)}, u32[]{:S(2)}, u32[]{:S(2)}) collective-permute-start(bf16[4,224,256]{2,1,0:T(8,128)(2,1)S(1)} %pad_maximum_fusion.refs_4_), channel_id=1, source_target_pairs={{0,16},{16,0},{1,17},{17,1},{2,18},{18,2},{3,19},{19,3},{4,20},{20... | collective-permute-start | bytes 1376264 | tf_op jit(solution)/shard_map/ppermute | solution.py:21
  21.1 1.5 collective-permute-start.7
  22.6 7.2 %collective-permute-done.10.refs_9_ = bf16[4,224,256]{2,1,0:T(8,128)(2,1)S(1)} collective-permute-done((bf16[4,224,256]{2,1,0:T(8,128)(2,1)S(1)}, bf16[4,224,256]{2,1,0:T(8,128)(2,1)S(1)}, u32[]{:S(2)}, u32[]{:S(2)}) %collective-permute-start.10) | collective-permute-done | bytes 458784 | tf_op jit(solution)/shard_map/ppermute | solution.py:21
  31.0 1.5 collective-permute-start.12
  32.4 2.0 %dynamic-slice_bitcast_fusion = (bf16[224,640]{1,0:T(8,128)(2,1)}, bf16[224,640]{1,0:T(8,128)(2,1)S(1)}, bf16[224,640]{1,0:T(8,128)(2,1)S(1)}, bf16[224,640]{1,0:T(8,128)(2,1)S(1)}) fusion(bf16[1,224,2560]{2,1,0:T(8,128)(2,1)} %param.7, s32[]{:T(128)S(6)} %select_n.31, s32[]{:T(128)S(6)} %select_n.29, s32[]{:T(128)S(6)} %select_n.28, s32[]{:T(128)S(6)} %select_n.30), kind=kLoop, calls=%fused_computation.1 | loop fusion | bytes 2293776 | tf_op jit(solution)/shard_map/dynamic_slice | solution.py:312
  34.6 2.7 %collective-permute-start.1 = (bf16[224,640]{1,0:T(8,128)(2,1)S(1)}, bf16[224,640]{1,0:T(8,128)(2,1)S(1)}, u32[]{:S(2)}, u32[]{:S(2)}) collective-permute-start(bf16[224,640]{1,0:T(8,128)(2,1)S(1)} %get-tuple-element.22), channel_id=1, source_target_pairs={{0,3},{1,0},{2,1},{3,2},{4,7},{5,4},{6,5},{7,6},{8,11},{9,8},{10,9... | collective-permute-start | bytes 860168 | tf_op jit(solution)/shard_map/ppermute | solution.py:21
  38.6 5.8 %collective-permute-done.11.refs_10_ = bf16[4,224,256]{2,1,0:T(8,128)(2,1)S(1)} collective-permute-done((bf16[4,224,256]{2,1,0:T(8,128)(2,1)S(1)}, bf16[4,224,256]{2,1,0:T(8,128)(2,1)S(1)}, u32[]{:S(2)}, u32[]{:S(2)}) %collective-permute-start.11) | collective-permute-done | bytes 458784 | tf_op jit(solution)/shard_map/ppermute | solution.py:21
  45.2 2.7 %collective-permute-start.9 = (bf16[2,224,256]{2,1,0:T(8,128)(2,1)}, bf16[2,224,256]{2,1,0:T(8,128)(2,1)}, u32[]{:S(2)}, u32[]{:S(2)}) collective-permute-start(bf16[2,224,256]{2,1,0:T(8,128)(2,1)} %slice.17), channel_id=1, source_target_pairs={{0,12},{4,0},{8,4},{12,8},{1,13},{5,1},{9,5},{13,9},{2,14},{6,2},{... | collective-permute-start | bytes 688136 | tf_op jit(solution)/shard_map/ppermute | solution.py:21
  49.3 2.7 %collective-permute-start.14 = (bf16[2,224,256]{2,1,0:T(8,128)(2,1)}, bf16[2,224,256]{2,1,0:T(8,128)(2,1)}, u32[]{:S(2)}, u32[]{:S(2)}) collective-permute-start(bf16[2,224,256]{2,1,0:T(8,128)(2,1)} %slice.19), channel_id=1, source_target_pairs={{0,12},{4,0},{8,4},{12,8},{1,13},{5,1},{9,5},{13,9},{2,14},{6,2},{... | collective-permute-start | bytes 688136 | tf_op jit(solution)/shard_map/ppermute | solution.py:21
  54.1 2.1 %collective-permute-done.8.refs_7_ = bf16[2,224,256]{2,1,0:T(8,128)(2,1)} collective-permute-done((bf16[2,224,256]{2,1,0:T(8,128)(2,1)}, bf16[2,224,256]{2,1,0:T(8,128)(2,1)}, u32[]{:S(2)}, u32[]{:S(2)}) %collective-permute-start.8) | collective-permute-done | bytes 229408 | tf_op jit(solution)/shard_map/ppermute | solution.py:21
  56.2 9.8 %collective-permute-done.13.refs_12_ = bf16[2,224,256]{2,1,0:T(8,128)(2,1)} collective-permute-done((bf16[2,224,256]{2,1,0:T(8,128)(2,1)}, bf16[2,224,256]{2,1,0:T(8,128)(2,1)}, u32[]{:S(2)}, u32[]{:S(2)}) %collective-permute-start.13) | collective-permute-done | bytes 229408 | tf_op jit(solution)/shard_map/ppermute | solution.py:21
  67.0 11.4 %attend.1 = (bf16[224,640]{1,0:T(8,128)(2,1)}, bf16[224,640]{1,0:T(8,128)(2,1)S(1)}, bf16[224,640]{1,0:T(8,128)(2,1)S(1)}, bf16[224,640]{1,0:T(8,128)(2,1)S(1)}) custom-call(s32[3]{0:T(128)S(1)} %pad_add_fusion.coords, s32[64]{0:T(128)S(1)} %copy-done.2, s32[64]{0:T(128)S(1)} %bitcast.37, s32[2]{0:T(128)S(1)} %pad_add_fusion.1.starts, ...), custom_call_target="tpu_custom_call" | custom-call | flops 8000000000 | bytes 6000000 | tf_op jit(solution)/shard_map/attend/pallas_call | solution.py:179
  78.5 2.7 %collective-permute-start.16 = (bf16[224,640]{1,0:T(8,128)(2,1)S(1)}, bf16[224,640]{1,0:T(8,128)(2,1)S(1)}, u32[]{:S(2)}, u32[]{:S(2)}) collective-permute-start(bf16[224,640]{1,0:T(8,128)(2,1)S(1)} %get-tuple-element.13), channel_id=1, source_target_pairs={{0,3},{1,0},{2,1},{3,2},{4,7},{5,4},{6,5},{7,6},{8,11},{9,8},{10,9... | collective-permute-start | bytes 860168 | tf_op jit(solution)/shard_map/ppermute | solution.py:21
  81.2 15.0 %collective-permute-start.18 = (bf16[224,640]{1,0:T(8,128)(2,1)}, bf16[224,640]{1,0:T(8,128)(2,1)S(1)}, u32[]{:S(2)}, u32[]{:S(2)}) collective-permute-start(bf16[224,640]{1,0:T(8,128)(2,1)} %get-tuple-element.11.refs_0_), channel_id=1, source_target_pairs={{0,32},{32,0},{1,33},{33,1},{2,34},{34,2},{3,35},{35,3},{4,36},{36... | collective-permute-start | bytes 860168 | tf_op jit(solution)/shard_map/ppermute | solution.py:21
  96.2 11.4 %collective-permute-start.19 = (bf16[224,640]{1,0:T(8,128)(2,1)S(1)}, bf16[224,640]{1,0:T(8,128)(2,1)S(1)}, u32[]{:S(2)}, u32[]{:S(2)}) collective-permute-start(bf16[224,640]{1,0:T(8,128)(2,1)S(1)} %collective-permute-done.15.refs_1_), channel_id=1, source_target_pairs={{0,32},{32,0},{1,33},{33,1},{2,34},{34,2},{3,35},{35,3},{4,36},{36... | collective-permute-start | bytes 860168 | tf_op jit(solution)/shard_map/ppermute | solution.py:21
  107.7 8.6 %collective-permute-start.21 = (bf16[224,640]{1,0:T(8,128)(2,1)S(1)}, bf16[224,640]{1,0:T(8,128)(2,1)S(1)}, u32[]{:S(2)}, u32[]{:S(2)}) collective-permute-start(bf16[224,640]{1,0:T(8,128)(2,1)S(1)} %collective-permute-done.17.refs_3_), channel_id=1, source_target_pairs={{0,32},{32,0},{1,33},{33,1},{2,34},{34,2},{3,35},{35,3},{4,36},{36... | collective-permute-start | bytes 860168 | tf_op jit(solution)/shard_map/ppermute | solution.py:21
  117.4 6.6 %all-gather.2.cloned.1.call-done.refs_8_ = bf16[5120,1280]{1,0:T(8,128)(2,1)} async-done(((bf16[80,1280]{1,0:T(8,128)(2,1)}), bf16[5120,1280]{1,0:T(8,128)(2,1)}) %all-gather.2.cloned.1.call-update) | async-done | bytes 13107216 | tf_op jit(solution)/shard_map/all_gather | solution.py:325
  124.0 12.1 %project.1 = (bf16[224,5120]{1,0:T(8,128)(2,1)}, bf16[2,224,1280]{2,1,0:T(8,128)(2,1)S(1)}) custom-call(s32[3]{0:T(128)S(1)} %pad_add_fusion.coords, s32[1]{0:T(128)} %bitcast.core, bf16[224,640]{1,0:T(8,128)(2,1)} %get-tuple-element.11.refs_0_, bf16[224,640]{1,0:T(8,128)(2,1)S(1)} %collective-permute-done.15.refs_1_, ...), custom_call_target="tpu_custom_call" | custom-call | flops 6000000000 | bytes 18000000 | tf_op jit(solution)/shard_map/project/pallas_call | solution.py:247
  136.8 2.4 %collective-permute-done.22.theirs = bf16[2,224,1280]{2,1,0:T(8,128)(2,1)S(1)} collective-permute-done((bf16[2,224,1280]{2,1,0:T(8,128)(2,1)S(1)}, bf16[2,224,1280]{2,1,0:T(8,128)(2,1)S(1)}, u32[]{:S(2)}, u32[]{:S(2)}) %collective-permute-start.22) | collective-permute-done | bytes 1146912 | tf_op jit(solution)/shard_map/ppermute | solution.py:21
  140.3 2.3 %merge.1 = bf16[224,5120]{1,0:T(8,128)(2,1)} custom-call(s32[1]{0:T(128)} %bitcast.core, bf16[2,224,1280]{2,1,0:T(8,128)(2,1)} %copy-done.4, bf16[224,5120]{1,0:T(8,128)(2,1)} %get-tuple-element.16.whole), custom_call_target="tpu_custom_call", output_to_operand_aliasing={{}: (2, {})} | custom-call | bytes 3000000 | tf_op jit(solution)/shard_map/merge/pallas_call | solution.py:285
  (54 shorter events, 15.0 us)
Async XLA Ops:
  6.5 117.5 %all-gather.2.cloned.1.call-start = ((), (), s32[]{:S(2)}) async-start(), calls=%async_computation | async-start | bytes 13312000 | tf_op jit(solution)/shard_map/all_gather | solution.py:325
  8.4 6.4 %collective-permute-start.3 = (bf16[224,256]{1,0:T(8,128)(2,1)S(1)}, bf16[224,256]{1,0:T(8,128)(2,1)S(1)}, u32[]{:S(2)}, u32[]{:S(2)}) collective-permute-start(bf16[224,256]{1,0:T(8,128)(2,1)S(1)} %pad_maximum_fusion.1), channel_id=1, source_target_pairs={{0,1},{1,2},{2,3},{3,0},{4,5},{5,6},{6,7},{7,4},{8,9},{9,10},{10,1... | collective-permute-start | bytes 344072 | tf_op jit(solution)/shard_map/ppermute | solution.py:21
  10.6 4.1 %collective-permute-start.4 = (bf16[224,256]{1,0:T(8,128)(2,1)S(1)}, bf16[224,256]{1,0:T(8,128)(2,1)S(1)}, u32[]{:S(2)}, u32[]{:S(2)}) collective-permute-start(bf16[224,256]{1,0:T(8,128)(2,1)S(1)} %pad_maximum_fusion.2), channel_id=1, source_target_pairs={{0,3},{1,0},{2,1},{3,2},{4,7},{5,4},{6,5},{7,6},{8,11},{9,8},{10,9... | collective-permute-start | bytes 344072 | tf_op jit(solution)/shard_map/ppermute | solution.py:21
  12.1 6.1 %collective-permute-start.5 = (bf16[224,256]{1,0:T(8,128)(2,1)S(1)}, bf16[224,256]{1,0:T(8,128)(2,1)S(1)}, u32[]{:S(2)}, u32[]{:S(2)}) collective-permute-start(bf16[224,256]{1,0:T(8,128)(2,1)S(1)} %pad_maximum_fusion.3), channel_id=1, source_target_pairs={{0,2},{1,3},{2,0},{3,1},{4,6},{5,7},{6,4},{7,5},{8,10},{9,11},{10,... | collective-permute-start | bytes 344072 | tf_op jit(solution)/shard_map/ppermute | solution.py:21
  18.3 11.5 %collective-permute-start.10 = (bf16[4,224,256]{2,1,0:T(8,128)(2,1)S(1)}, bf16[4,224,256]{2,1,0:T(8,128)(2,1)S(1)}, u32[]{:S(2)}, u32[]{:S(2)}) collective-permute-start(bf16[4,224,256]{2,1,0:T(8,128)(2,1)S(1)} %pad_maximum_fusion.refs_4_), channel_id=1, source_target_pairs={{0,16},{16,0},{1,17},{17,1},{2,18},{18,2},{3,19},{19,3},{4,20},{20... | collective-permute-start | bytes 1376264 | tf_op jit(solution)/shard_map/ppermute | solution.py:21
  19.9 14.6 %collective-permute-start.6 = (bf16[4,224,256]{2,1,0:T(8,128)(2,1)S(1)}, bf16[4,224,256]{2,1,0:T(8,128)(2,1)S(1)}, u32[]{:S(2)}, u32[]{:S(2)}) collective-permute-start(bf16[4,224,256]{2,1,0:T(8,128)(2,1)S(1)} %pad_maximum_fusion.refs_4_), channel_id=1, source_target_pairs={{0,4},{4,8},{8,12},{12,0},{1,5},{5,9},{9,13},{13,1},{2,6},{6,10},{... | collective-permute-start | bytes 1376264 | tf_op jit(solution)/shard_map/ppermute | solution.py:21
  21.1 16.8 %collective-permute-start.7 = (bf16[4,224,256]{2,1,0:T(8,128)(2,1)S(1)}, bf16[4,224,256]{2,1,0:T(8,128)(2,1)S(1)}, u32[]{:S(2)}, u32[]{:S(2)}) collective-permute-start(bf16[4,224,256]{2,1,0:T(8,128)(2,1)S(1)} %pad_maximum_fusion.refs_4_), channel_id=1, source_target_pairs={{0,12},{4,0},{8,4},{12,8},{1,13},{5,1},{9,5},{13,9},{2,14},{6,2},{... | collective-permute-start | bytes 1376264 | tf_op jit(solution)/shard_map/ppermute | solution.py:21
  29.8 14.7 %collective-permute-start.11 = (bf16[4,224,256]{2,1,0:T(8,128)(2,1)S(1)}, bf16[4,224,256]{2,1,0:T(8,128)(2,1)S(1)}, u32[]{:S(2)}, u32[]{:S(2)}) collective-permute-start(bf16[4,224,256]{2,1,0:T(8,128)(2,1)S(1)} %collective-permute-done.10.refs_9_), channel_id=1, source_target_pairs={{0,4},{4,8},{8,12},{12,0},{1,5},{5,9},{9,13},{13,1},{2,6},{6,10},{... | collective-permute-start | bytes 1376264 | tf_op jit(solution)/shard_map/ppermute | solution.py:21
  31.0 14.2 %collective-permute-start.12 = (bf16[4,224,256]{2,1,0:T(8,128)(2,1)S(1)}, bf16[4,224,256]{2,1,0:T(8,128)(2,1)S(1)}, u32[]{:S(2)}, u32[]{:S(2)}) collective-permute-start(bf16[4,224,256]{2,1,0:T(8,128)(2,1)S(1)} %collective-permute-done.10.refs_9_), channel_id=1, source_target_pairs={{0,12},{4,0},{8,4},{12,8},{1,13},{5,1},{9,5},{13,9},{2,14},{6,2},{... | collective-permute-start | bytes 1376264 | tf_op jit(solution)/shard_map/ppermute | solution.py:21
  34.5 14.1 %collective-permute-start = (bf16[224,640]{1,0:T(8,128)(2,1)S(1)}, bf16[224,640]{1,0:T(8,128)(2,1)S(1)}, u32[]{:S(2)}, u32[]{:S(2)}) collective-permute-start(bf16[224,640]{1,0:T(8,128)(2,1)S(1)} %get-tuple-element.20), channel_id=1, source_target_pairs={{0,1},{1,2},{2,3},{3,0},{4,5},{5,6},{6,7},{7,4},{8,9},{9,10},{10,1... | collective-permute-start | bytes 860168 | tf_op jit(solution)/shard_map/ppermute | solution.py:21
  34.6 14.0 %collective-permute-start.1 = (bf16[224,640]{1,0:T(8,128)(2,1)S(1)}, bf16[224,640]{1,0:T(8,128)(2,1)S(1)}, u32[]{:S(2)}, u32[]{:S(2)}) collective-permute-start(bf16[224,640]{1,0:T(8,128)(2,1)S(1)} %get-tuple-element.22), channel_id=1, source_target_pairs={{0,3},{1,0},{2,1},{3,2},{4,7},{5,4},{6,5},{7,6},{8,11},{9,8},{10,9... | collective-permute-start | bytes 860168 | tf_op jit(solution)/shard_map/ppermute | solution.py:21
  37.9 16.2 %collective-permute-start.2 = (bf16[224,640]{1,0:T(8,128)(2,1)}, bf16[224,640]{1,0:T(8,128)(2,1)}, u32[]{:S(2)}, u32[]{:S(2)}) collective-permute-start(bf16[224,640]{1,0:T(8,128)(2,1)} %get-tuple-element.19), channel_id=1, source_target_pairs={{0,2},{1,3},{2,0},{3,1},{4,6},{5,7},{6,4},{7,5},{8,10},{9,11},{10,... | collective-permute-start | bytes 860168 | tf_op jit(solution)/shard_map/ppermute | solution.py:21
  44.5 11.8 %collective-permute-start.8 = (bf16[2,224,256]{2,1,0:T(8,128)(2,1)}, bf16[2,224,256]{2,1,0:T(8,128)(2,1)}, u32[]{:S(2)}, u32[]{:S(2)}) collective-permute-start(bf16[2,224,256]{2,1,0:T(8,128)(2,1)} %slice.16), channel_id=1, source_target_pairs={{0,4},{4,8},{8,12},{12,0},{1,5},{5,9},{9,13},{13,1},{2,6},{6,10},{... | collective-permute-start | bytes 688136 | tf_op jit(solution)/shard_map/ppermute | solution.py:21
  45.2 11.0 %collective-permute-start.9 = (bf16[2,224,256]{2,1,0:T(8,128)(2,1)}, bf16[2,224,256]{2,1,0:T(8,128)(2,1)}, u32[]{:S(2)}, u32[]{:S(2)}) collective-permute-start(bf16[2,224,256]{2,1,0:T(8,128)(2,1)} %slice.17), channel_id=1, source_target_pairs={{0,12},{4,0},{8,4},{12,8},{1,13},{5,1},{9,5},{13,9},{2,14},{6,2},{... | collective-permute-start | bytes 688136 | tf_op jit(solution)/shard_map/ppermute | solution.py:21
  48.6 17.5 %collective-permute-start.13 = (bf16[2,224,256]{2,1,0:T(8,128)(2,1)}, bf16[2,224,256]{2,1,0:T(8,128)(2,1)}, u32[]{:S(2)}, u32[]{:S(2)}) collective-permute-start(bf16[2,224,256]{2,1,0:T(8,128)(2,1)} %slice.18), channel_id=1, source_target_pairs={{0,4},{4,8},{8,12},{12,0},{1,5},{5,9},{9,13},{13,1},{2,6},{6,10},{... | collective-permute-start | bytes 688136 | tf_op jit(solution)/shard_map/ppermute | solution.py:21
  49.3 16.8 %collective-permute-start.14 = (bf16[2,224,256]{2,1,0:T(8,128)(2,1)}, bf16[2,224,256]{2,1,0:T(8,128)(2,1)}, u32[]{:S(2)}, u32[]{:S(2)}) collective-permute-start(bf16[2,224,256]{2,1,0:T(8,128)(2,1)} %slice.19), channel_id=1, source_target_pairs={{0,12},{4,0},{8,4},{12,8},{1,13},{5,1},{9,5},{13,9},{2,14},{6,2},{... | collective-permute-start | bytes 688136 | tf_op jit(solution)/shard_map/ppermute | solution.py:21
  78.5 17.7 %collective-permute-start.15 = (bf16[224,640]{1,0:T(8,128)(2,1)S(1)}, bf16[224,640]{1,0:T(8,128)(2,1)S(1)}, u32[]{:S(2)}, u32[]{:S(2)}) collective-permute-start(bf16[224,640]{1,0:T(8,128)(2,1)S(1)} %get-tuple-element.12), channel_id=1, source_target_pairs={{0,1},{1,2},{2,3},{3,0},{4,5},{5,6},{6,7},{7,4},{8,9},{9,10},{10,1... | collective-permute-start | bytes 860168 | tf_op jit(solution)/shard_map/ppermute | solution.py:21
  78.5 29.1 %collective-permute-start.16 = (bf16[224,640]{1,0:T(8,128)(2,1)S(1)}, bf16[224,640]{1,0:T(8,128)(2,1)S(1)}, u32[]{:S(2)}, u32[]{:S(2)}) collective-permute-start(bf16[224,640]{1,0:T(8,128)(2,1)S(1)} %get-tuple-element.13), channel_id=1, source_target_pairs={{0,3},{1,0},{2,1},{3,2},{4,7},{5,4},{6,5},{7,6},{8,11},{9,8},{10,9... | collective-permute-start | bytes 860168 | tf_op jit(solution)/shard_map/ppermute | solution.py:21
  81.2 26.4 %collective-permute-start.17 = (bf16[224,640]{1,0:T(8,128)(2,1)S(1)}, bf16[224,640]{1,0:T(8,128)(2,1)S(1)}, u32[]{:S(2)}, u32[]{:S(2)}) collective-permute-start(bf16[224,640]{1,0:T(8,128)(2,1)S(1)} %get-tuple-element.14), channel_id=1, source_target_pairs={{0,2},{1,3},{2,0},{3,1},{4,6},{5,7},{6,4},{7,5},{8,10},{9,11},{10,... | collective-permute-start | bytes 860168 | tf_op jit(solution)/shard_map/ppermute | solution.py:21
  81.2 35.0 %collective-permute-start.18 = (bf16[224,640]{1,0:T(8,128)(2,1)}, bf16[224,640]{1,0:T(8,128)(2,1)S(1)}, u32[]{:S(2)}, u32[]{:S(2)}) collective-permute-start(bf16[224,640]{1,0:T(8,128)(2,1)} %get-tuple-element.11.refs_0_), channel_id=1, source_target_pairs={{0,32},{32,0},{1,33},{33,1},{2,34},{34,2},{3,35},{35,3},{4,36},{36... | collective-permute-start | bytes 860168 | tf_op jit(solution)/shard_map/ppermute | solution.py:21
  96.2 20.0 %collective-permute-start.19 = (bf16[224,640]{1,0:T(8,128)(2,1)S(1)}, bf16[224,640]{1,0:T(8,128)(2,1)S(1)}, u32[]{:S(2)}, u32[]{:S(2)}) collective-permute-start(bf16[224,640]{1,0:T(8,128)(2,1)S(1)} %collective-permute-done.15.refs_1_), channel_id=1, source_target_pairs={{0,32},{32,0},{1,33},{33,1},{2,34},{34,2},{3,35},{35,3},{4,36},{36... | collective-permute-start | bytes 860168 | tf_op jit(solution)/shard_map/ppermute | solution.py:21
  107.6 8.6 %collective-permute-start.20 = (bf16[224,640]{1,0:T(8,128)(2,1)S(1)}, bf16[224,640]{1,0:T(8,128)(2,1)S(1)}, u32[]{:S(2)}, u32[]{:S(2)}) collective-permute-start(bf16[224,640]{1,0:T(8,128)(2,1)S(1)} %collective-permute-done.16.refs_2_), channel_id=1, source_target_pairs={{0,32},{32,0},{1,33},{33,1},{2,34},{34,2},{3,35},{35,3},{4,36},{36... | collective-permute-start | bytes 860168 | tf_op jit(solution)/shard_map/ppermute | solution.py:21
  107.7 9.8 %collective-permute-start.21 = (bf16[224,640]{1,0:T(8,128)(2,1)S(1)}, bf16[224,640]{1,0:T(8,128)(2,1)S(1)}, u32[]{:S(2)}, u32[]{:S(2)}) collective-permute-start(bf16[224,640]{1,0:T(8,128)(2,1)S(1)} %collective-permute-done.17.refs_3_), channel_id=1, source_target_pairs={{0,32},{32,0},{1,33},{33,1},{2,34},{34,2},{3,35},{35,3},{4,36},{36... | collective-permute-start | bytes 860168 | tf_op jit(solution)/shard_map/ppermute | solution.py:21
  136.1 3.2 %collective-permute-start.22 = (bf16[2,224,1280]{2,1,0:T(8,128)(2,1)S(1)}, bf16[2,224,1280]{2,1,0:T(8,128)(2,1)S(1)}, u32[]{:S(2)}, u32[]{:S(2)}) collective-permute-start(bf16[2,224,1280]{2,1,0:T(8,128)(2,1)S(1)} %get-tuple-element.15), channel_id=1, source_target_pairs={{0,32},{32,0},{1,33},{33,1},{2,34},{34,2},{3,35},{35,3},{4,36},{36... | collective-permute-start | bytes 3440648 | tf_op jit(solution)/shard_map/ppermute | solution.py:21
  (6 other events, 83.3 us)
Sparse Core Ops, SparseCore 0:
  10.2 113.7 all-gather.1
